TPU v7x, 128 devices: a whole 4x4x4 slice. The times are simulated.
128 devices in a mesh: ctx: 16 (over z_hi, y, core), head: 8 (over x, z_lo).
Axes of the slice: x: 4, y: 4, z: 4 (z_hi: 2, z_lo: 2; z = z_hi * 2 + z_lo), core: 2. Of those that a mesh axis runs over, the one named last changes fastest.
Arguments:
- queries: bfloat16 [4096, 5120], P('ctx', 'head'), may hold values from -6 to 6
- key_matrix_rows: bfloat16 [4096, 5120], P('ctx', 'head'), may hold values from -6 to 6
- value_matrix_rows: bfloat16 [4096, 5120], P('ctx', 'head'), may hold values from -6 to 6
- attention_output: bfloat16 [4096, 5120], P('ctx', 'head'), may hold values from -6 to 6
- output_gradient: bfloat16 [4096, 5120], P('ctx', 'head'), may hold values from -96 to 96
- log_sum_norm: float32 [40, 4096], P('head', 'ctx'), may hold values from 6 to 8
- features: bfloat16 [4096, 5120], P('ctx', 'head'), may hold values from -6 to 6
- adapter_down_weight: bfloat16 [3, 5120, 128], P(None, 'head'), may hold values from -0.078125 to 0.078125
- adapter_up_weight: bfloat16 [3, 128, 5120], P(None, None, 'head'), may hold values from -0.078125 to 0.078125
- attended_key_blocks: int32 [32, 16], P('ctx'), may hold values from 0 to 31, as said below
- used_block_count: int32 [32], P('ctx'), may hold values from 1 to 16, as said below
Outputs:
- query_grad: bfloat16 [4096, 5120], P('ctx', 'head')
- key_grad: bfloat16 [4096, 5120], P('ctx', 'head')
- value_grad: bfloat16 [4096, 5120], P('ctx', 'head')
- down_matrix_gradient: float32 [3, 5120, 128], P(None, 'head')
- up_matrix_gradient: float32 [3, 128, 5120], P(None, None, 'head')
Inputs may be any that keep to these rules, and one draw needn't show every extreme that they name: `attended_key_blocks`: entries 0 to used_block_count[b] - 1 of row b are distinct, entry 0 is b itself, and the unused entries repeat entry 0. `used_block_count`: some row uses all 16 entries.
All inputs are finite; a program needn't handle non-finite values.
Results may differ from a plain program's by a relative error of at most 0.0058.
Values may be sent and summed in bfloat16 or wider, within the bound.
A program may use at most 64 MiB of HBM per device.

v0:
```python
import jax
import jax.numpy as jnp
from jax import lax
from jax.sharding import PartitionSpec as P

BLOCK = 128


adapter_scale = 0.125


def passed_along(value, axis, steps):
    count = lax.axis_size(axis)
    pairs = [(source, (source + steps) % count) for source in range(count)]
    return lax.ppermute(value, axis, pairs)


def shortened(value):

    def short(part):
        return part.astype(jnp.bfloat16) if part.dtype == jnp.float32 else part

    return jax.tree.map(short, value)


def expand_mask(block_mask):
    return jnp.repeat(jnp.repeat(block_mask, BLOCK, axis=0), BLOCK, axis=1) > 0.5


def attend(
    queries, key_matrix_rows, value_matrix_rows, output_gradient, log_sum_norm, row_dot, block_mask
):
    head_count = log_sum_norm.shape[0]
    query_count = queries.shape[0]
    key_count = key_matrix_rows.shape[0]
    head_size = queries.shape[1] // head_count
    scaling = head_size ** (-0.5)
    query_heads = queries.reshape(query_count, head_count, head_size)
    key_heads = key_matrix_rows.reshape(key_count, head_count, head_size)
    value_heads = value_matrix_rows.reshape(key_count, head_count, head_size)
    grad_heads = output_gradient.reshape(query_count, head_count, head_size)

    def compute(unused):
        scores = jnp.einsum(
            "qhd,khd->hqk", query_heads, key_heads, preferred_element_type=jnp.float32
        )
        live_mask = expand_mask(block_mask)
        weights = jnp.where(
            live_mask[None], jnp.exp(scores * scaling - log_sum_norm[:, :, None]), 0.0
        )
        value_dot = jnp.einsum(
            "qhd,khd->hqk", grad_heads, value_heads, preferred_element_type=jnp.float32
        )
        score_grad = (weights * (value_dot - row_dot[:, :, None]) * scaling).astype(jnp.bfloat16)
        results = []
        query_part = jnp.einsum(
            "hqk,khd->qhd", score_grad, key_heads, preferred_element_type=jnp.float32
        )
        results.append(query_part.reshape(query_count, head_count * head_size))
        weights_low = weights.astype(jnp.bfloat16)
        value_part = jnp.einsum(
            "hqk,qhd->khd", weights_low, grad_heads, preferred_element_type=jnp.float32
        )
        key_part = jnp.einsum(
            "hqk,qhd->khd", score_grad, query_heads, preferred_element_type=jnp.float32
        )
        results.append(
            jnp.concatenate(
                [
                    key_part.reshape(key_count, head_count * head_size),
                    value_part.reshape(key_count, head_count * head_size),
                ],
                axis=1,
            )
        )
        return tuple(results)

    def skipped(unused):
        outputs = []
        outputs.append(jnp.zeros((query_count, head_count * head_size), jnp.float32))
        outputs.append(jnp.zeros((key_count, 2 * head_count * head_size), jnp.float32))
        return tuple(outputs)

    return lax.cond(jnp.any(block_mask > 0.5), compute, skipped, 0)


def on_device(
    queries,
    key_matrix_rows,
    value_matrix_rows,
    attention_output,
    output_gradient,
    log_sum_norm,
    features,
    adapter_down_weight,
    adapter_up_weight,
    attended_key_blocks,
    used_block_count,
):
    position = lax.axis_index("ctx")
    cycle_size = lax.axis_size("ctx")
    token_count = queries.shape[0]
    head_count = log_sum_norm.shape[0]
    col_count = queries.shape[1]
    local_blocks = attended_key_blocks.shape[0]
    slot_count = attended_key_blocks.shape[1]
    block_total = local_blocks * cycle_size
    row_dot = (
        (output_gradient.astype(jnp.float32) * attention_output.astype(jnp.float32))
        .reshape(token_count, head_count, col_count // head_count)
        .sum(axis=2)
        .T
    )
    valid_slots = jnp.arange(slot_count)[None, :] < used_block_count[:, None]
    matches = (
        attended_key_blocks[:, :, None] == jnp.arange(block_total, dtype=jnp.int32)[None, None, :]
    ) & valid_slots[:, :, None]
    block_mask = jnp.any(matches, axis=1).astype(jnp.float32)

    def columns(rows_mask, source):
        return lax.dynamic_slice_in_dim(rows_mask, source * local_blocks, local_blocks, 1)

    down_piece = jnp.einsum(
        "vc,fco->fvo", features, adapter_down_weight, preferred_element_type=jnp.float32
    )
    projected_rows = lax.psum(down_piece, "head").astype(jnp.bfloat16)
    query_acc, key_acc = attend(
        queries,
        key_matrix_rows,
        value_matrix_rows,
        output_gradient,
        log_sum_norm,
        row_dot,
        columns(block_mask, position),
    )

    def carried_turn(turn, state):
        query_sum, held_keys, held_values, key_sum = state
        held_keys, held_values = passed_along((held_keys, held_values), "ctx", 1)
        key_sum = passed_along(key_sum, "ctx", 1)
        source = (position - turn) % cycle_size
        query_add, key_add = attend(
            queries,
            held_keys,
            held_values,
            output_gradient,
            log_sum_norm,
            row_dot,
            columns(block_mask, source),
        )
        return (query_sum + query_add, held_keys, held_values, key_sum + key_add)

    query_acc, spent_keys, spent_values, key_acc = lax.fori_loop(
        1, cycle_size, carried_turn, (query_acc, key_matrix_rows, value_matrix_rows, key_acc)
    )
    key_acc = jax.tree.map(
        lambda part, own: part.astype(own.dtype),
        passed_along(shortened(key_acc), "ctx", 1),
        key_acc,
    )
    query_grad = query_acc.astype(jnp.bfloat16)
    key_grad = key_acc[:, :col_count].astype(jnp.bfloat16)
    value_grad = key_acc[:, col_count:].astype(jnp.bfloat16)
    shifted_rows = jnp.stack([query_grad, key_grad, value_grad])
    head_piece = jnp.einsum(
        "oki,oji->okj", shifted_rows, adapter_up_weight, preferred_element_type=jnp.float32
    )
    collected_rows = lax.psum(head_piece, "head").astype(jnp.bfloat16)
    up_piece = adapter_scale * jnp.einsum(
        "pjf,pjd->pfd", projected_rows, shifted_rows, preferred_element_type=jnp.float32
    )
    down_piece_gradient = adapter_scale * jnp.einsum(
        "sq,ysw->yqw", features, collected_rows, preferred_element_type=jnp.float32
    )
    down_matrix_gradient, up_matrix_gradient = lax.psum((down_piece_gradient, up_piece), "ctx")
    return (query_grad, key_grad, value_grad, down_matrix_gradient, up_matrix_gradient)


def solution(mesh):
    placed = (
        P("ctx", "head"),
        P("ctx", "head"),
        P("ctx", "head"),
        P("ctx", "head"),
        P("ctx", "head"),
        P("head", "ctx"),
        P("ctx", "head"),
        P(None, "head", None),
        P(None, None, "head"),
        P("ctx", None),
        P("ctx"),
    )
    return jax.shard_map(
        on_device,
        mesh=mesh,
        in_specs=placed,
        out_specs=(
            P("ctx", "head"),
            P("ctx", "head"),
            P("ctx", "head"),
            P(None, "head", None),
            P(None, None, "head"),
        ),
        check_vma=False,
    )
```

profile of v0, /device:TPU:1, one launch (start us, length us, event | category | flops | bytes accessed | tf_op | source)
XLA Modules:
  0.0 798.3 jit_solution(7817195027631804644)
XLA Ops:
  15.5 7.2 conditional.2
  22.7 537.4 %while.21 = (s32[]{:T(128)}, f32[256,640]{0,1:T(8,128)}, bf16[256,640]{0,1:T(8,128)(2,1)}, bf16[256,640]{0,1:T(8,128)(2,1)}, f32[256,1280]{0,1:T(8,128)}, /*inde...) while((s32[]{:T(128)}, f32[256,640]{0,1:T(8,128)}, ...), condition=%wide.region_9.10_spmd, body=%wide.region_5.9_spmd.sunk | while | flops 422871072 | bytes 29438608 | solution.py:153
  28.5 15.2 %collective-permute-done = bf16[256,640]{0,1:T(8,128)(2,1)S(1)} collective-permute-done((bf16[256,640]{0,1:T(8,128)(2,1)}, bf16[256,640]{0,1:T(8,128)(2,1)S(1)}, u32[]{:S(2)}, u32[]{:S(2)}) %collective-permute-start) | collective-permute-done | bytes 327712 | tf_op jit(solution)/shard_map/while/body/eval_jaxpr/ppermute | solution.py:15
  47.3 3.8 conditional.4
  62.7 15.2 %collective-permute-done = bf16[256,640]{0,1:T(8,128)(2,1)S(1)} collective-permute-done((bf16[256,640]{0,1:T(8,128)(2,1)}, bf16[256,640]{0,1:T(8,128)(2,1)S(1)}, u32[]{:S(2)}, u32[]{:S(2)}) %collective-permute-start) | collective-permute-done | bytes 327712 | tf_op jit(solution)/shard_map/while/body/eval_jaxpr/ppermute | solution.py:15
  87.9 6.0 collective-permute-start.2
  95.3 16.9 %collective-permute-done = bf16[256,640]{0,1:T(8,128)(2,1)S(1)} collective-permute-done((bf16[256,640]{0,1:T(8,128)(2,1)}, bf16[256,640]{0,1:T(8,128)(2,1)S(1)}, u32[]{:S(2)}, u32[]{:S(2)}) %collective-permute-start) | collective-permute-done | bytes 327712 | tf_op jit(solution)/shard_map/while/body/eval_jaxpr/ppermute | solution.py:15
  115.7 3.8 conditional.4
  129.6 16.9 %collective-permute-done = bf16[256,640]{0,1:T(8,128)(2,1)S(1)} collective-permute-done((bf16[256,640]{0,1:T(8,128)(2,1)}, bf16[256,640]{0,1:T(8,128)(2,1)S(1)}, u32[]{:S(2)}, u32[]{:S(2)}) %collective-permute-start) | collective-permute-done | bytes 327712 | tf_op jit(solution)/shard_map/while/body/eval_jaxpr/ppermute | solution.py:15
  150.0 3.8 conditional.4
  163.8 16.9 %collective-permute-done = bf16[256,640]{0,1:T(8,128)(2,1)S(1)} collective-permute-done((bf16[256,640]{0,1:T(8,128)(2,1)}, bf16[256,640]{0,1:T(8,128)(2,1)S(1)}, u32[]{:S(2)}, u32[]{:S(2)}) %collective-permute-start) | collective-permute-done | bytes 327712 | tf_op jit(solution)/shard_map/while/body/eval_jaxpr/ppermute | solution.py:15
  184.2 3.8 conditional.4
  198.0 16.9 %collective-permute-done = bf16[256,640]{0,1:T(8,128)(2,1)S(1)} collective-permute-done((bf16[256,640]{0,1:T(8,128)(2,1)}, bf16[256,640]{0,1:T(8,128)(2,1)S(1)}, u32[]{:S(2)}, u32[]{:S(2)}) %collective-permute-start) | collective-permute-done | bytes 327712 | tf_op jit(solution)/shard_map/while/body/eval_jaxpr/ppermute | solution.py:15
  224.8 6.0 collective-permute-start.2
  232.2 17.7 %collective-permute-done = bf16[256,640]{0,1:T(8,128)(2,1)S(1)} collective-permute-done((bf16[256,640]{0,1:T(8,128)(2,1)}, bf16[256,640]{0,1:T(8,128)(2,1)S(1)}, u32[]{:S(2)}, u32[]{:S(2)}) %collective-permute-start) | collective-permute-done | bytes 327712 | tf_op jit(solution)/shard_map/while/body/eval_jaxpr/ppermute | solution.py:15
  252.7 3.8 conditional.4
  266.5 21.3 %collective-permute-done = bf16[256,640]{0,1:T(8,128)(2,1)S(1)} collective-permute-done((bf16[256,640]{0,1:T(8,128)(2,1)}, bf16[256,640]{0,1:T(8,128)(2,1)S(1)}, u32[]{:S(2)}, u32[]{:S(2)}) %collective-permute-start) | collective-permute-done | bytes 327712 | tf_op jit(solution)/shard_map/while/body/eval_jaxpr/ppermute | solution.py:15
  300.2 21.8 %collective-permute-done = bf16[256,640]{0,1:T(8,128)(2,1)S(1)} collective-permute-done((bf16[256,640]{0,1:T(8,128)(2,1)}, bf16[256,640]{0,1:T(8,128)(2,1)S(1)}, u32[]{:S(2)}, u32[]{:S(2)}) %collective-permute-start) | collective-permute-done | bytes 327712 | tf_op jit(solution)/shard_map/while/body/eval_jaxpr/ppermute | solution.py:15
  323.0 3.8 conditional.4
  333.0 3.8 collective-permute-start.1
  338.2 21.7 %collective-permute-done = bf16[256,640]{0,1:T(8,128)(2,1)S(1)} collective-permute-done((bf16[256,640]{0,1:T(8,128)(2,1)}, bf16[256,640]{0,1:T(8,128)(2,1)S(1)}, u32[]{:S(2)}, u32[]{:S(2)}) %collective-permute-start) | collective-permute-done | bytes 327712 | tf_op jit(solution)/shard_map/while/body/eval_jaxpr/ppermute | solution.py:15
  360.8 3.8 conditional.4
  372.3 25.5 %collective-permute-done = bf16[256,640]{0,1:T(8,128)(2,1)S(1)} collective-permute-done((bf16[256,640]{0,1:T(8,128)(2,1)}, bf16[256,640]{0,1:T(8,128)(2,1)S(1)}, u32[]{:S(2)}, u32[]{:S(2)}) %collective-permute-start) | collective-permute-done | bytes 327712 | tf_op jit(solution)/shard_map/while/body/eval_jaxpr/ppermute | solution.py:15
  398.7 3.8 conditional.4
  410.3 25.3 %collective-permute-done = bf16[256,640]{0,1:T(8,128)(2,1)S(1)} collective-permute-done((bf16[256,640]{0,1:T(8,128)(2,1)}, bf16[256,640]{0,1:T(8,128)(2,1)S(1)}, u32[]{:S(2)}, u32[]{:S(2)}) %collective-permute-start) | collective-permute-done | bytes 327712 | tf_op jit(solution)/shard_map/while/body/eval_jaxpr/ppermute | solution.py:15
  436.5 3.8 conditional.4
  448.2 25.3 %collective-permute-done = bf16[256,640]{0,1:T(8,128)(2,1)S(1)} collective-permute-done((bf16[256,640]{0,1:T(8,128)(2,1)}, bf16[256,640]{0,1:T(8,128)(2,1)S(1)}, u32[]{:S(2)}, u32[]{:S(2)}) %collective-permute-start) | collective-permute-done | bytes 327712 | tf_op jit(solution)/shard_map/while/body/eval_jaxpr/ppermute | solution.py:15
  486.0 25.3 %collective-permute-done = bf16[256,640]{0,1:T(8,128)(2,1)S(1)} collective-permute-done((bf16[256,640]{0,1:T(8,128)(2,1)}, bf16[256,640]{0,1:T(8,128)(2,1)S(1)}, u32[]{:S(2)}, u32[]{:S(2)}) %collective-permute-start) | collective-permute-done | bytes 327712 | tf_op jit(solution)/shard_map/while/body/eval_jaxpr/ppermute | solution.py:15
  523.9 25.3 %collective-permute-done = bf16[256,640]{0,1:T(8,128)(2,1)S(1)} collective-permute-done((bf16[256,640]{0,1:T(8,128)(2,1)}, bf16[256,640]{0,1:T(8,128)(2,1)S(1)}, u32[]{:S(2)}, u32[]{:S(2)}) %collective-permute-start) | collective-permute-done | bytes 327712 | tf_op jit(solution)/shard_map/while/body/eval_jaxpr/ppermute | solution.py:15
  563.5 25.0 %collective-permute-done.3 = bf16[256,1280]{1,0:T(8,128)(2,1)S(1)} collective-permute-done((bf16[256,1280]{1,0:T(8,128)(2,1)S(1)}, bf16[256,1280]{1,0:T(8,128)(2,1)S(1)}, u32[]{:S(2)}, u32[]{:S(2)}) %collective-permute-start.3) | collective-permute-done | bytes 655392 | tf_op jit(solution)/shard_map/ppermute | solution.py:15
  589.0 44.8 %all-reduce.6 = (bf16[3,256,128]{2,1,0:T(8,128)(2,1)S(1)}, bf16[3,256,128]{1,2,0:T(8,128)(2,1)S(1)}) all-reduce(f32[3,256,128]{2,1,0:T(8,128)S(1)} %fusion.17, f32[3,256,128]{1,2,0:T(8,128)S(1)} %convolution_bitcast_fusion), channel_id=1, replica_groups=mesh['ctx'=16,'head'=8] {'head'}, use_global_device_ids=true, to_apply=%region_10.11 | all-reduce | flops 196608 | bytes 1179648 | tf_op jit(solution)/shard_map/psum | solution.py:168
  636.5 151.5 %all-reduce.5.cloned.1.call-done = (f32[3,640,128]{1,2,0:T(8,128)}, f32[3,128,640]{2,1,0:T(8,128)}) async-done(((f32[3,640,128]{1,2,0:T(8,128)}, f32[3,128,640]{2,1,0:T(8,128)}), (f32[3,640,128]{1,2,0:T(8,128)}, f32[3,128,640]{2,1,0:T(8,128)})) %all-reduce.5.cloned.1.call-update) | async-done | bytes 1966096 | tf_op jit(solution)/shard_map/psum | solution.py:175
  (421 shorter events, 244.2 us)
Async XLA Ops:
  7.2 780.7 %all-reduce.5.cloned.1.call-start = ((), (), s32[]{:S(2)}) async-start(), calls=%async_computation | async-start | bytes 3932160 | tf_op jit(solution)/shard_map/psum | solution.py:175
  22.7 31.8 %collective-permute-start.2 = (f32[256,1280]{0,1:T(8,128)}, f32[256,1280]{0,1:T(8,128)}, u32[]{:S(2)}, u32[]{:S(2)}) collective-permute-start(f32[256,1280]{0,1:T(8,128)} %get-tuple-element.528), channel_id=1, source_target_pairs={{0,8},{8,16},{16,24},{24,32},{32,40},{40,48},{48,56},{56,64},{64,7... | collective-permute-start | bytes 3932168 | tf_op jit(solution)/shard_map/while/body/eval_jaxpr/ppermute | solution.py:15
  57.2 27.9 %collective-permute-start.2 = (f32[256,1280]{0,1:T(8,128)}, f32[256,1280]{0,1:T(8,128)}, u32[]{:S(2)}, u32[]{:S(2)}) collective-permute-start(f32[256,1280]{0,1:T(8,128)} %get-tuple-element.528), channel_id=1, source_target_pairs={{0,8},{8,16},{16,24},{24,32},{32,40},{40,48},{48,56},{56,64},{64,7... | collective-permute-start | bytes 3932168 | tf_op jit(solution)/shard_map/while/body/eval_jaxpr/ppermute | solution.py:15
  87.9 35.1 %collective-permute-start.2 = (f32[256,1280]{0,1:T(8,128)}, f32[256,1280]{0,1:T(8,128)}, u32[]{:S(2)}, u32[]{:S(2)}) collective-permute-start(f32[256,1280]{0,1:T(8,128)} %get-tuple-element.528), channel_id=1, source_target_pairs={{0,8},{8,16},{16,24},{24,32},{32,40},{40,48},{48,56},{56,64},{64,7... | collective-permute-start | bytes 3932168 | tf_op jit(solution)/shard_map/while/body/eval_jaxpr/ppermute | solution.py:15
  125.7 31.5 %collective-permute-start.2 = (f32[256,1280]{0,1:T(8,128)}, f32[256,1280]{0,1:T(8,128)}, u32[]{:S(2)}, u32[]{:S(2)}) collective-permute-start(f32[256,1280]{0,1:T(8,128)} %get-tuple-element.528), channel_id=1, source_target_pairs={{0,8},{8,16},{16,24},{24,32},{32,40},{40,48},{48,56},{56,64},{64,7... | collective-permute-start | bytes 3932168 | tf_op jit(solution)/shard_map/while/body/eval_jaxpr/ppermute | solution.py:15
  159.9 31.5 %collective-permute-start.2 = (f32[256,1280]{0,1:T(8,128)}, f32[256,1280]{0,1:T(8,128)}, u32[]{:S(2)}, u32[]{:S(2)}) collective-permute-start(f32[256,1280]{0,1:T(8,128)} %get-tuple-element.528), channel_id=1, source_target_pairs={{0,8},{8,16},{16,24},{24,32},{32,40},{40,48},{48,56},{56,64},{64,7... | collective-permute-start | bytes 3932168 | tf_op jit(solution)/shard_map/while/body/eval_jaxpr/ppermute | solution.py:15
  194.2 27.9 %collective-permute-start.2 = (f32[256,1280]{0,1:T(8,128)}, f32[256,1280]{0,1:T(8,128)}, u32[]{:S(2)}, u32[]{:S(2)}) collective-permute-start(f32[256,1280]{0,1:T(8,128)} %get-tuple-element.528), channel_id=1, source_target_pairs={{0,8},{8,16},{16,24},{24,32},{32,40},{40,48},{48,56},{56,64},{64,7... | collective-permute-start | bytes 3932168 | tf_op jit(solution)/shard_map/while/body/eval_jaxpr/ppermute | solution.py:15
  224.8 35.1 %collective-permute-start.2 = (f32[256,1280]{0,1:T(8,128)}, f32[256,1280]{0,1:T(8,128)}, u32[]{:S(2)}, u32[]{:S(2)}) collective-permute-start(f32[256,1280]{0,1:T(8,128)} %get-tuple-element.528), channel_id=1, source_target_pairs={{0,8},{8,16},{16,24},{24,32},{32,40},{40,48},{48,56},{56,64},{64,7... | collective-permute-start | bytes 3932168 | tf_op jit(solution)/shard_map/while/body/eval_jaxpr/ppermute | solution.py:15
  262.6 33.4 %collective-permute-start.2 = (f32[256,1280]{0,1:T(8,128)}, f32[256,1280]{0,1:T(8,128)}, u32[]{:S(2)}, u32[]{:S(2)}) collective-permute-start(f32[256,1280]{0,1:T(8,128)} %get-tuple-element.528), channel_id=1, source_target_pairs={{0,8},{8,16},{16,24},{24,32},{32,40},{40,48},{48,56},{56,64},{64,7... | collective-permute-start | bytes 3932168 | tf_op jit(solution)/shard_map/while/body/eval_jaxpr/ppermute | solution.py:15
  265.0 23.7 %collective-permute-start.1 = (bf16[256,640]{0,1:T(8,128)(2,1)}, bf16[256,640]{0,1:T(8,128)(2,1)S(1)}, u32[]{:S(2)}, u32[]{:S(2)}) collective-permute-start(bf16[256,640]{0,1:T(8,128)(2,1)} %get-tuple-element.527), channel_id=1, source_target_pairs={{0,8},{8,16},{16,24},{24,32},{32,40},{40,48},{48,56},{56,64},{64,7... | collective-permute-start | bytes 983048 | tf_op jit(solution)/shard_map/while/body/eval_jaxpr/ppermute | solution.py:15
  298.7 31.5 %collective-permute-start.2 = (f32[256,1280]{0,1:T(8,128)}, f32[256,1280]{0,1:T(8,128)}, u32[]{:S(2)}, u32[]{:S(2)}) collective-permute-start(f32[256,1280]{0,1:T(8,128)} %get-tuple-element.528), channel_id=1, source_target_pairs={{0,8},{8,16},{16,24},{24,32},{32,40},{40,48},{48,56},{56,64},{64,7... | collective-permute-start | bytes 3932168 | tf_op jit(solution)/shard_map/while/body/eval_jaxpr/ppermute | solution.py:15
  298.7 23.3 %collective-permute-start = (bf16[256,640]{0,1:T(8,128)(2,1)}, bf16[256,640]{0,1:T(8,128)(2,1)S(1)}, u32[]{:S(2)}, u32[]{:S(2)}) collective-permute-start(bf16[256,640]{0,1:T(8,128)(2,1)} %get-tuple-element.526), channel_id=1, source_target_pairs={{0,8},{8,16},{16,24},{24,32},{32,40},{40,48},{48,56},{56,64},{64,7... | collective-permute-start | bytes 983048 | tf_op jit(solution)/shard_map/while/body/eval_jaxpr/ppermute | solution.py:15
  298.7 24.3 %collective-permute-start.1 = (bf16[256,640]{0,1:T(8,128)(2,1)}, bf16[256,640]{0,1:T(8,128)(2,1)S(1)}, u32[]{:S(2)}, u32[]{:S(2)}) collective-permute-start(bf16[256,640]{0,1:T(8,128)(2,1)} %get-tuple-element.527), channel_id=1, source_target_pairs={{0,8},{8,16},{16,24},{24,32},{32,40},{40,48},{48,56},{56,64},{64,7... | collective-permute-start | bytes 983048 | tf_op jit(solution)/shard_map/while/body/eval_jaxpr/ppermute | solution.py:15
  332.9 35.1 %collective-permute-start.2 = (f32[256,1280]{0,1:T(8,128)}, f32[256,1280]{0,1:T(8,128)}, u32[]{:S(2)}, u32[]{:S(2)}) collective-permute-start(f32[256,1280]{0,1:T(8,128)} %get-tuple-element.528), channel_id=1, source_target_pairs={{0,8},{8,16},{16,24},{24,32},{32,40},{40,48},{48,56},{56,64},{64,7... | collective-permute-start | bytes 3932168 | tf_op jit(solution)/shard_map/while/body/eval_jaxpr/ppermute | solution.py:15
  333.0 26.9 %collective-permute-start = (bf16[256,640]{0,1:T(8,128)(2,1)}, bf16[256,640]{0,1:T(8,128)(2,1)S(1)}, u32[]{:S(2)}, u32[]{:S(2)}) collective-permute-start(bf16[256,640]{0,1:T(8,128)(2,1)} %get-tuple-element.526), channel_id=1, source_target_pairs={{0,8},{8,16},{16,24},{24,32},{32,40},{40,48},{48,56},{56,64},{64,7... | collective-permute-start | bytes 983048 | tf_op jit(solution)/shard_map/while/body/eval_jaxpr/ppermute | solution.py:15
  333.0 27.9 %collective-permute-start.1 = (bf16[256,640]{0,1:T(8,128)(2,1)}, bf16[256,640]{0,1:T(8,128)(2,1)S(1)}, u32[]{:S(2)}, u32[]{:S(2)}) collective-permute-start(bf16[256,640]{0,1:T(8,128)(2,1)} %get-tuple-element.527), channel_id=1, source_target_pairs={{0,8},{8,16},{16,24},{24,32},{32,40},{40,48},{48,56},{56,64},{64,7... | collective-permute-start | bytes 983048 | tf_op jit(solution)/shard_map/while/body/eval_jaxpr/ppermute | solution.py:15
  370.8 35.1 %collective-permute-start.2 = (f32[256,1280]{0,1:T(8,128)}, f32[256,1280]{0,1:T(8,128)}, u32[]{:S(2)}, u32[]{:S(2)}) collective-permute-start(f32[256,1280]{0,1:T(8,128)} %get-tuple-element.528), channel_id=1, source_target_pairs={{0,8},{8,16},{16,24},{24,32},{32,40},{40,48},{48,56},{56,64},{64,7... | collective-permute-start | bytes 3932168 | tf_op jit(solution)/shard_map/while/body/eval_jaxpr/ppermute | solution.py:15
  370.8 26.9 %collective-permute-start = (bf16[256,640]{0,1:T(8,128)(2,1)}, bf16[256,640]{0,1:T(8,128)(2,1)S(1)}, u32[]{:S(2)}, u32[]{:S(2)}) collective-permute-start(bf16[256,640]{0,1:T(8,128)(2,1)} %get-tuple-element.526), channel_id=1, source_target_pairs={{0,8},{8,16},{16,24},{24,32},{32,40},{40,48},{48,56},{56,64},{64,7... | collective-permute-start | bytes 983048 | tf_op jit(solution)/shard_map/while/body/eval_jaxpr/ppermute | solution.py:15
  370.8 27.9 %collective-permute-start.1 = (bf16[256,640]{0,1:T(8,128)(2,1)}, bf16[256,640]{0,1:T(8,128)(2,1)S(1)}, u32[]{:S(2)}, u32[]{:S(2)}) collective-permute-start(bf16[256,640]{0,1:T(8,128)(2,1)} %get-tuple-element.527), channel_id=1, source_target_pairs={{0,8},{8,16},{16,24},{24,32},{32,40},{40,48},{48,56},{56,64},{64,7... | collective-permute-start | bytes 983048 | tf_op jit(solution)/shard_map/while/body/eval_jaxpr/ppermute | solution.py:15
  408.7 35.1 %collective-permute-start.2 = (f32[256,1280]{0,1:T(8,128)}, f32[256,1280]{0,1:T(8,128)}, u32[]{:S(2)}, u32[]{:S(2)}) collective-permute-start(f32[256,1280]{0,1:T(8,128)} %get-tuple-element.528), channel_id=1, source_target_pairs={{0,8},{8,16},{16,24},{24,32},{32,40},{40,48},{48,56},{56,64},{64,7... | collective-permute-start | bytes 3932168 | tf_op jit(solution)/shard_map/while/body/eval_jaxpr/ppermute | solution.py:15
  408.7 26.9 %collective-permute-start = (bf16[256,640]{0,1:T(8,128)(2,1)}, bf16[256,640]{0,1:T(8,128)(2,1)S(1)}, u32[]{:S(2)}, u32[]{:S(2)}) collective-permute-start(bf16[256,640]{0,1:T(8,128)(2,1)} %get-tuple-element.526), channel_id=1, source_target_pairs={{0,8},{8,16},{16,24},{24,32},{32,40},{40,48},{48,56},{56,64},{64,7... | collective-permute-start | bytes 983048 | tf_op jit(solution)/shard_map/while/body/eval_jaxpr/ppermute | solution.py:15
  408.7 27.9 %collective-permute-start.1 = (bf16[256,640]{0,1:T(8,128)(2,1)}, bf16[256,640]{0,1:T(8,128)(2,1)S(1)}, u32[]{:S(2)}, u32[]{:S(2)}) collective-permute-start(bf16[256,640]{0,1:T(8,128)(2,1)} %get-tuple-element.527), channel_id=1, source_target_pairs={{0,8},{8,16},{16,24},{24,32},{32,40},{40,48},{48,56},{56,64},{64,7... | collective-permute-start | bytes 983048 | tf_op jit(solution)/shard_map/while/body/eval_jaxpr/ppermute | solution.py:15
  446.5 35.1 %collective-permute-start.2 = (f32[256,1280]{0,1:T(8,128)}, f32[256,1280]{0,1:T(8,128)}, u32[]{:S(2)}, u32[]{:S(2)}) collective-permute-start(f32[256,1280]{0,1:T(8,128)} %get-tuple-element.528), channel_id=1, source_target_pairs={{0,8},{8,16},{16,24},{24,32},{32,40},{40,48},{48,56},{56,64},{64,7... | collective-permute-start | bytes 3932168 | tf_op jit(solution)/shard_map/while/body/eval_jaxpr/ppermute | solution.py:15
  446.5 26.9 %collective-permute-start = (bf16[256,640]{0,1:T(8,128)(2,1)}, bf16[256,640]{0,1:T(8,128)(2,1)S(1)}, u32[]{:S(2)}, u32[]{:S(2)}) collective-permute-start(bf16[256,640]{0,1:T(8,128)(2,1)} %get-tuple-element.526), channel_id=1, source_target_pairs={{0,8},{8,16},{16,24},{24,32},{32,40},{40,48},{48,56},{56,64},{64,7... | collective-permute-start | bytes 983048 | tf_op jit(solution)/shard_map/while/body/eval_jaxpr/ppermute | solution.py:15
  446.5 27.9 %collective-permute-start.1 = (bf16[256,640]{0,1:T(8,128)(2,1)}, bf16[256,640]{0,1:T(8,128)(2,1)S(1)}, u32[]{:S(2)}, u32[]{:S(2)}) collective-permute-start(bf16[256,640]{0,1:T(8,128)(2,1)} %get-tuple-element.527), channel_id=1, source_target_pairs={{0,8},{8,16},{16,24},{24,32},{32,40},{40,48},{48,56},{56,64},{64,7... | collective-permute-start | bytes 983048 | tf_op jit(solution)/shard_map/while/body/eval_jaxpr/ppermute | solution.py:15
  484.4 35.1 %collective-permute-start.2 = (f32[256,1280]{0,1:T(8,128)}, f32[256,1280]{0,1:T(8,128)}, u32[]{:S(2)}, u32[]{:S(2)}) collective-permute-start(f32[256,1280]{0,1:T(8,128)} %get-tuple-element.528), channel_id=1, source_target_pairs={{0,8},{8,16},{16,24},{24,32},{32,40},{40,48},{48,56},{56,64},{64,7... | collective-permute-start | bytes 3932168 | tf_op jit(solution)/shard_map/while/body/eval_jaxpr/ppermute | solution.py:15
  484.4 26.9 %collective-permute-start = (bf16[256,640]{0,1:T(8,128)(2,1)}, bf16[256,640]{0,1:T(8,128)(2,1)S(1)}, u32[]{:S(2)}, u32[]{:S(2)}) collective-permute-start(bf16[256,640]{0,1:T(8,128)(2,1)} %get-tuple-element.526), channel_id=1, source_target_pairs={{0,8},{8,16},{16,24},{24,32},{32,40},{40,48},{48,56},{56,64},{64,7... | collective-permute-start | bytes 983048 | tf_op jit(solution)/shard_map/while/body/eval_jaxpr/ppermute | solution.py:15
  484.4 27.9 %collective-permute-start.1 = (bf16[256,640]{0,1:T(8,128)(2,1)}, bf16[256,640]{0,1:T(8,128)(2,1)S(1)}, u32[]{:S(2)}, u32[]{:S(2)}) collective-permute-start(bf16[256,640]{0,1:T(8,128)(2,1)} %get-tuple-element.527), channel_id=1, source_target_pairs={{0,8},{8,16},{16,24},{24,32},{32,40},{40,48},{48,56},{56,64},{64,7... | collective-permute-start | bytes 983048 | tf_op jit(solution)/shard_map/while/body/eval_jaxpr/ppermute | solution.py:15
  522.2 35.1 %collective-permute-start.2 = (f32[256,1280]{0,1:T(8,128)}, f32[256,1280]{0,1:T(8,128)}, u32[]{:S(2)}, u32[]{:S(2)}) collective-permute-start(f32[256,1280]{0,1:T(8,128)} %get-tuple-element.528), channel_id=1, source_target_pairs={{0,8},{8,16},{16,24},{24,32},{32,40},{40,48},{48,56},{56,64},{64,7... | collective-permute-start | bytes 3932168 | tf_op jit(solution)/shard_map/while/body/eval_jaxpr/ppermute | solution.py:15
  522.2 26.9 %collective-permute-start = (bf16[256,640]{0,1:T(8,128)(2,1)}, bf16[256,640]{0,1:T(8,128)(2,1)S(1)}, u32[]{:S(2)}, u32[]{:S(2)}) collective-permute-start(bf16[256,640]{0,1:T(8,128)(2,1)} %get-tuple-element.526), channel_id=1, source_target_pairs={{0,8},{8,16},{16,24},{24,32},{32,40},{40,48},{48,56},{56,64},{64,7... | collective-permute-start | bytes 983048 | tf_op jit(solution)/shard_map/while/body/eval_jaxpr/ppermute | solution.py:15
  522.2 27.9 %collective-permute-start.1 = (bf16[256,640]{0,1:T(8,128)(2,1)}, bf16[256,640]{0,1:T(8,128)(2,1)S(1)}, u32[]{:S(2)}, u32[]{:S(2)}) collective-permute-start(bf16[256,640]{0,1:T(8,128)(2,1)} %get-tuple-element.527), channel_id=1, source_target_pairs={{0,8},{8,16},{16,24},{24,32},{32,40},{40,48},{48,56},{56,64},{64,7... | collective-permute-start | bytes 983048 | tf_op jit(solution)/shard_map/while/body/eval_jaxpr/ppermute | solution.py:15
  561.7 26.8 %collective-permute-start.3 = (bf16[256,1280]{1,0:T(8,128)(2,1)S(1)}, bf16[256,1280]{1,0:T(8,128)(2,1)S(1)}, u32[]{:S(2)}, u32[]{:S(2)}) collective-permute-start(bf16[256,1280]{1,0:T(8,128)(2,1)S(1)} %copy.79), channel_id=1, source_target_pairs={{0,8},{8,16},{16,24},{24,32},{32,40},{40,48},{48,56},{56,64},{64,7... | collective-permute-start | bytes 1966088 | tf_op jit(solution)/shard_map/ppermute | solution.py:15
  (41 other events, 1086.4 us)
Sparse Core Ops, SparseCore 0:
  636.6 151.2 all-reduce.4
where the time goes:
time: 800 us; the launch traced here: 798 us
  waiting for transfers between devices  515 us (64%)
  other arithmetic  85.8 us (11%)
  local copies, waits for them, and re-layouts  49.2 us (6%)
  blocking collectives  44.8 us (6%)
  matrix products  43.3 us (5%)
  starting transfers between devices  35 us (4%)
  between operations  14.9 us (2%)
  loops' own time  10.3 us (1%)
    ppermute x46, waiting for transfers between devices, passed_along(): return lax.ppermute(value, axis, pairs)  364 us
    psum x1, waiting for transfers between devices, on_device(): lax.psum((down_piece_gradient, up_piece), 'ctx')  151 us
    add x30, other arithmetic, carried_turn(): return (query_sum + query_add, held_keys, held_values, key_sum + key_add)  71.4 us
    psum x1, blocking collectives, on_device(): collected_rows = lax.psum(head_piece, 'head').astype(jnp.bfloat16)  44.8 us
    ppermute x46, starting transfers between devices, passed_along(): return lax.ppermute(value, axis, pairs)  34.9 us
    while x30, local copies, waits for them, and re-layouts  21.7 us
    dot_general x14, matrix products, compute(): jnp.einsum('qhd,khd->hqk', query_heads, key_heads, preferred_element_type...  20.7 us
  transfers between devices with their start and end apart: 47, of which 32 were waited for; matrix products, arithmetic and copies ran while one was open for 13% of the time, Pallas kernels for 0%

commit v1 on v0

v1 whole, which is shorter than its diff:
```python
import functools
import math

import jax
import jax.numpy as jnp
from jax import lax
from jax.experimental import pallas as pl
from jax.experimental.pallas import tpu as pltpu
from jax.sharding import PartitionSpec as P

MESH = pl.DeviceIdType.MESH
BF16 = jnp.bfloat16
F32 = jnp.float32

HEADS = 5
WIDTH = 128
TOKENS = 256
RING = 16
PARTS = 2
SPAN = RING // PARTS
KEYS = SPAN * TOKENS
TILE = 256
WORKERS = HEADS * PARTS
SCALE = WIDTH ** -0.5
LOG2E = math.log2(math.e)
DEAD = 1e30
adapter_scale = 0.125


def nt(a, b):
    return lax.dot_general(a, b, (((1,), (1,)), ((), ())), preferred_element_type=F32)


def nn(a, b):
    return lax.dot_general(a, b, (((1,), (0,)), ((), ())), preferred_element_type=F32)


def lane_slice(h):
    return pl.ds(pl.multiple_of(h * WIDTH, WIDTH), WIDTH)


def attention_kernel(
    q_ref, k_ref, v_ref, o_ref, g_ref, lse_ref, att_ref, used_ref,
    qg_ref, kg_ref, vg_ref,
    stats, rq, rg, rs, rk, rv, kt_buf, dk_acc, dv_acc, dq_acc,
    dqs, dks, dvs, rdq, rdk, rdv,
    q_send, g_send, s_send, k_send, v_send, dq_send, dk_send, dv_send,
    q_recv, g_recv, s_recv, k_recv, v_recv, dq_recv, dk_recv, dv_recv,
):
    me = lax.axis_index("ctx")
    group = lax.axis_index("head")

    def move(src, dst, send_sem, recv_sem, target):
        return pltpu.make_async_remote_copy(
            src_ref=src, dst_ref=dst, send_sem=send_sem, recv_sem=recv_sem,
            device_id=(target, group), device_id_type=MESH,
        )

    def start(src, dst, send_sem, recv_sem, target):
        @pl.when(target != me)
        def _():
            move(src, dst, send_sem, recv_sem, target).start()

        @pl.when(target == me)
        def _():
            pltpu.make_async_copy(src, dst, recv_sem).start()

    def sent(src, dst, send_sem, recv_sem, target):
        @pl.when(target != me)
        def _():
            move(src, dst, send_sem, recv_sem, target).wait_send()

    def landed(dst, recv_sem):
        pltpu.make_async_copy(dst, dst, recv_sem).wait()

    barrier = pltpu.get_barrier_semaphore()

    def greet(step, carry):
        pl.semaphore_signal(
            barrier, inc=1, device_id=(lax.rem(me + step, RING), group), device_id_type=MESH
        )
        return carry

    lax.fori_loop(1, RING, greet, 0)
    pl.semaphore_wait(barrier, RING - 1)

    my_part = me // SPAN
    my_place = lax.rem(me, SPAN)

    def kv_copies(h):
        target = h * PARTS + my_part
        rows = pl.ds(pl.multiple_of(my_place * TOKENS, TOKENS), TOKENS)
        return (
            (k_ref.at[:, lane_slice(h)], rk.at[rows], k_send.at[h], k_recv.at[my_place], target),
            (v_ref.at[:, lane_slice(h)], rv.at[rows], v_send.at[h], v_recv.at[my_place], target),
        )

    def send_kv(step, carry):
        h = lax.rem(step + me, HEADS)
        for copy in kv_copies(h):
            start(*copy)
        return carry

    lax.fori_loop(0, HEADS, send_kv, 0)

    lane = lax.broadcasted_iota(jnp.int32, (1, TOKENS), 1)
    codes = []
    for part in range(PARTS):
        words = []
        for row in range(2):
            word = jnp.int32(0)
            for slot in range(16):
                block = att_ref[row, slot] - part * 2 * SPAN
                inside = (block >= 0) & (block < 2 * SPAN) & (slot < used_ref[row])
                bit = jnp.left_shift(jnp.int32(1), jnp.clip(block, 0, 2 * SPAN - 1))
                word = word | jnp.where(inside, bit, 0)
            words.append(word)
        codes.append(jnp.where(lane < TOKENS // 2, words[0], words[1]).astype(F32))
    for h in range(HEADS):
        columns = slice(h * WIDTH, (h + 1) * WIDTH)
        product = g_ref[:, columns].astype(F32) * o_ref[:, columns].astype(F32)
        row_dot = jnp.sum(product.T, axis=0, keepdims=True)
        norm = lse_ref[h : h + 1, :] * LOG2E - math.log2(SCALE)
        for part in range(PARTS):
            stats[h * PARTS + part] = jnp.concatenate(
                [norm, row_dot, codes[part], jnp.zeros((5, TOKENS), F32)], axis=0
            )

    def query_copies(target):
        h = target // PARTS
        return (
            (stats.at[target], rs.at[me], s_send.at[target], s_recv.at[me], target),
            (q_ref.at[:, lane_slice(h)], rq.at[me], q_send.at[target], q_recv.at[me], target),
            (g_ref.at[:, lane_slice(h)], rg.at[me], g_send.at[target], g_recv.at[me], target),
        )

    def send_queries(step, carry):
        target = lax.rem(me + step, RING)

        @pl.when(target < WORKERS)
        def _():
            for copy in query_copies(target):
                start(*copy)

        return carry

    lax.fori_loop(0, RING, send_queries, 0)

    my_head = me // PARTS
    work_part = lax.rem(me, PARTS)

    def dq_copy(source):
        return (dqs.at[source], rdq.at[me], dq_send.at[source], dq_recv.at[me], source)

    def key_copies(place):
        target = work_part * SPAN + place
        rows = pl.ds(pl.multiple_of(place * TOKENS, TOKENS), TOKENS)
        return (
            (dks.at[rows], rdk.at[my_head], dk_send.at[place], dk_recv.at[my_head], target),
            (dvs.at[rows], rdv.at[my_head], dv_send.at[place], dv_recv.at[my_head], target),
        )

    @pl.when(me < WORKERS)
    def _work():
        def keys_in(place, carry):
            rows = pl.ds(pl.multiple_of(place * TOKENS, TOKENS), TOKENS)
            landed(rk.at[rows], k_recv.at[place])
            landed(rv.at[rows], v_recv.at[place])
            kt_buf[:, rows] = rk[rows].astype(F32).T.astype(BF16)
            dk_acc[rows] = jnp.zeros((TOKENS, WIDTH), F32)
            dv_acc[rows] = jnp.zeros((TOKENS, WIDTH), F32)
            return carry

        lax.fori_loop(0, SPAN, keys_in, 0)

        def one_source(step, carry):
            source = lax.rem(me - step + RING, RING)
            landed(rs.at[source], s_recv.at[source])
            landed(rq.at[source], q_recv.at[source])
            landed(rg.at[source], g_recv.at[source])
            queries = rq[source]
            grads = rg[source]
            norm = rs[source, 0:1, :]
            row_dot = rs[source, 1:2, :]
            code = rs[source, 2:3, :].astype(jnp.int32)
            dq_acc[...] = jnp.zeros_like(dq_acc)

            def one_tile(tile, inner):
                rows = pl.ds(pl.multiple_of(tile * TILE, TILE), TILE)
                keys = rk[rows]
                scores = nt(keys, queries)
                value_dot = nt(rv[rows], grads)
                low_parts, grad_parts = [], []
                for sub in range(TILE // 128):
                    bit = jnp.right_shift(code, tile * (TILE // 128) + sub) & 1
                    bias = jnp.where(bit > 0, norm, DEAD)
                    piece = slice(sub * 128, (sub + 1) * 128)
                    weights = jnp.exp2(scores[piece] * (SCALE * LOG2E) - bias)
                    low_parts.append(weights.astype(BF16))
                    grad_parts.append((weights * (value_dot[piece] - row_dot)).astype(BF16))
                low = jnp.concatenate(low_parts, axis=0)
                score_grad = jnp.concatenate(grad_parts, axis=0)
                dv_acc[rows] += nn(low, grads)
                dk_acc[rows] += nn(score_grad, queries)
                dq_acc[...] += nn(kt_buf[:, rows], score_grad)
                return inner

            lax.fori_loop(0, KEYS // TILE, one_tile, 0, unroll=2)
            dqs[source] = dq_acc[...].T.astype(BF16)
            start(*dq_copy(source))
            return carry

        lax.fori_loop(0, RING, one_source, 0)

        def keys_out(place, carry):
            rows = pl.ds(pl.multiple_of(place * TOKENS, TOKENS), TOKENS)
            dks[rows] = dk_acc[rows].astype(BF16)
            dvs[rows] = (dv_acc[rows] * (1.0 / SCALE)).astype(BF16)
            for copy in key_copies(place):
                start(*copy)
            return carry

        lax.fori_loop(0, SPAN, keys_out, 0)

    for h in range(HEADS):
        columns = slice(h * WIDTH, (h + 1) * WIDTH)
        total = None
        for part in range(PARTS):
            slot = h * PARTS + part
            landed(rdq.at[slot], dq_recv.at[slot])
            piece = rdq[slot].astype(F32)
            total = piece if total is None else total + piece
        qg_ref[:, columns] = total.astype(BF16)
    for h in range(HEADS):
        columns = slice(h * WIDTH, (h + 1) * WIDTH)
        landed(rdk.at[h], dk_recv.at[h])
        kg_ref[:, columns] = rdk[h]
        landed(rdv.at[h], dv_recv.at[h])
        vg_ref[:, columns] = rdv[h]

    def drain_kv(h, carry):
        for copy in kv_copies(h):
            sent(*copy)
        return carry

    lax.fori_loop(0, HEADS, drain_kv, 0)

    def drain_queries(target, carry):
        for copy in query_copies(target):
            sent(*copy)
        return carry

    lax.fori_loop(0, WORKERS, drain_queries, 0)

    @pl.when(me < WORKERS)
    def _drain():
        def drain_dq(source, carry):
            sent(*dq_copy(source))
            return carry

        lax.fori_loop(0, RING, drain_dq, 0)

        def drain_keys(place, carry):
            for copy in key_copies(place):
                sent(*copy)
            return carry

        lax.fori_loop(0, SPAN, drain_keys, 0)


def attention(queries, keys, values, output, grads, norm, blocks, used):
    vmem = pl.BlockSpec(memory_space=pltpu.VMEM)
    smem = pl.BlockSpec(memory_space=pltpu.SMEM)
    rows = jax.ShapeDtypeStruct((TOKENS, HEADS * WIDTH), BF16)
    dma = pltpu.SemaphoreType.DMA
    return pl.pallas_call(
        attention_kernel,
        out_shape=(rows, rows, rows),
        in_specs=[vmem] * 6 + [smem] * 2,
        out_specs=(vmem, vmem, vmem),
        scratch_shapes=[
            pltpu.VMEM((WORKERS, 8, TOKENS), F32),
            pltpu.VMEM((RING, TOKENS, WIDTH), BF16),
            pltpu.VMEM((RING, TOKENS, WIDTH), BF16),
            pltpu.VMEM((RING, 8, TOKENS), F32),
            pltpu.VMEM((KEYS, WIDTH), BF16),
            pltpu.VMEM((KEYS, WIDTH), BF16),
            pltpu.VMEM((WIDTH, KEYS), BF16),
            pltpu.VMEM((KEYS, WIDTH), F32),
            pltpu.VMEM((KEYS, WIDTH), F32),
            pltpu.VMEM((WIDTH, TOKENS), F32),
            pltpu.VMEM((RING, TOKENS, WIDTH), BF16),
            pltpu.VMEM((KEYS, WIDTH), BF16),
            pltpu.VMEM((KEYS, WIDTH), BF16),
            pltpu.VMEM((WORKERS, TOKENS, WIDTH), BF16),
            pltpu.VMEM((HEADS, TOKENS, WIDTH), BF16),
            pltpu.VMEM((HEADS, TOKENS, WIDTH), BF16),
            dma((WORKERS,)), dma((WORKERS,)), dma((WORKERS,)), dma((HEADS,)), dma((HEADS,)),
            dma((RING,)), dma((SPAN,)), dma((SPAN,)),
            dma((RING,)), dma((RING,)), dma((RING,)), dma((SPAN,)), dma((SPAN,)),
            dma((WORKERS,)), dma((HEADS,)), dma((HEADS,)),
        ],
        compiler_params=pltpu.CompilerParams(
            collective_id=0, has_side_effects=True, vmem_limit_bytes=48 * 2**20
        ),
        name="attention",
    )(queries, keys, values, output, grads, norm, blocks, used)


def on_device(
    queries,
    key_matrix_rows,
    value_matrix_rows,
    attention_output,
    output_gradient,
    log_sum_norm,
    features,
    adapter_down_weight,
    adapter_up_weight,
    attended_key_blocks,
    used_block_count,
):
    down_piece = jnp.einsum(
        "vc,fco->fvo", features, adapter_down_weight, preferred_element_type=jnp.float32
    )
    projected_rows = lax.psum(down_piece, "head").astype(jnp.bfloat16)
    query_grad, key_grad, value_grad = attention(
        queries, key_matrix_rows, value_matrix_rows, attention_output, output_gradient,
        log_sum_norm, attended_key_blocks, used_block_count,
    )
    shifted_rows = jnp.stack([query_grad, key_grad, value_grad])
    head_piece = jnp.einsum(
        "oki,oji->okj", shifted_rows, adapter_up_weight, preferred_element_type=jnp.float32
    )
    collected_rows = lax.psum(head_piece, "head").astype(jnp.bfloat16)
    up_piece = adapter_scale * jnp.einsum(
        "pjf,pjd->pfd", projected_rows, shifted_rows, preferred_element_type=jnp.float32
    )
    down_piece_gradient = adapter_scale * jnp.einsum(
        "sq,ysw->yqw", features, collected_rows, preferred_element_type=jnp.float32
    )
    down_matrix_gradient, up_matrix_gradient = lax.psum((down_piece_gradient, up_piece), "ctx")
    return (query_grad, key_grad, value_grad, down_matrix_gradient, up_matrix_gradient)


def solution(mesh):
    placed = (
        P("ctx", "head"),
        P("ctx", "head"),
        P("ctx", "head"),
        P("ctx", "head"),
        P("ctx", "head"),
        P("head", "ctx"),
        P("ctx", "head"),
        P(None, "head", None),
        P(None, None, "head"),
        P("ctx", None),
        P("ctx"),
    )
    return jax.shard_map(
        on_device,
        mesh=mesh,
        in_specs=placed,
        out_specs=(
            P("ctx", "head"),
            P("ctx", "head"),
            P("ctx", "head"),
            P(None, "head", None),
            P(None, None, "head"),
        ),
        check_vma=False,
    )
```

time: 800 us -> 311 us (0.39)
  waiting for transfers between devices: 515 us -> 149 us
  Pallas kernels: 0 us -> 95.9 us
  other arithmetic: 85.8 us -> 0 us
  local copies, waits for them, and re-layouts: 49.2 us -> 8.5 us
  matrix products: 43.3 us -> 4.33 us
  starting transfers between devices: 35 us -> 0.04 us
  loops' own time: 10.3 us -> 0 us
    ppermute x46 -> x0, waiting for transfers between devices: 364 us -> none  [passed_along(): return lax.ppermute(value, axis, pairs)]
    pallas_call x0 -> x1, Pallas kernels: none -> 95.9 us  [attention(): pl.pallas_call(attention_kernel, out_shape=(rows, rows, rows), in_specs=[...]
    add x30 -> x0, other arithmetic: 71.4 us -> none  [carried_turn(): return (query_sum + query_add, held_keys, held_values, key_sum + key_add)]
    dot_general x70 -> x0, matrix products: 39.9 us -> none  [the longest x14 20.7 us: compute(): jnp.einsum('qhd,khd->hqk', query_heads, key_heads, preferred_element_type...]
    ppermute x46 -> x0, starting transfers between devices: 34.9 us -> none  [passed_along(): return lax.ppermute(value, axis, pairs)]
    while x35 -> x0, local copies, waits for them, and re-layouts: 27.3 us -> none
    reduce_or x17 -> x0, other arithmetic: 11.1 us -> none  [the longest x16 10.4 us: attend(): return lax.cond(jnp.any(block_mask > 0.5), compute, skipped, 0)]
    another operation x17 -> x0, loops' own time: 10.3 us -> none  [the longest x1 9.52 us: on_device(): lax.fori_loop(1, cycle_size, carried_turn, (query_acc, key_matrix_rows, v...]
  transfers between devices with their start and end apart: 47 -> 1, of which waited for: 32 -> 1; matrix products, arithmetic and copies ran while one was open for 13% -> 0% of each run, Pallas kernels for 0% -> 0%
where the time goes in v1:
time: 311 us
  waiting for transfers between devices  149 us (48%)
  Pallas kernels  95.9 us (31%)
  blocking collectives  38.4 us (12%)
  between operations  14.2 us (5%)
  local copies, waits for them, and re-layouts  8.5 us (3%)
  matrix products  4.33 us (1%)
    psum x1, waiting for transfers between devices, on_device(): lax.psum((down_piece_gradient, up_piece), 'ctx')  149 us
    pallas_call x1, Pallas kernels, attention(): pl.pallas_call(attention_kernel, out_shape=(rows, rows, rows), in_specs=[...  95.9 us
    psum x1, blocking collectives, on_device(): collected_rows = lax.psum(head_piece, 'head').astype(jnp.bfloat16)  38.4 us
    unnamed x29, local copies, waits for them, and re-layouts  8.5 us
  transfers between devices with their start and end apart: 1, of which 1 were waited for; matrix products, arithmetic and copies ran while one was open for 0% of the time, Pallas kernels for 0%

profile of v1, /device:TPU:1, one launch (start us, length us, event | category | flops | bytes accessed | tf_op | source)
XLA Modules:
  0.0 310.6 jit_solution(13333094953308911043)
XLA Ops:
  7.2 0.0 copy-start
  7.2 0.0 copy-start.8
  7.2 0.0 copy-start.7
  7.2 0.0 copy-start.6
  7.2 0.0 copy-start.3
  7.2 0.0 copy-start.2
  7.2 0.0 copy-start.1
  7.2 0.0 all-reduce.5.cloned.1.call-start
  7.3 0.9 copy-done
  8.2 1.3 convolution_bitcast_fusion
  9.5 0.0 copy-done.8
  9.6 0.0 copy-done.7
  9.6 0.0 copy-done.6
  9.6 0.0 copy-done.3
  9.6 0.0 copy-done.2
  9.6 0.0 copy-start.4
  9.6 1.0 copy-done.4
  10.6 1.0 copy-done.5
  11.6 95.9 %attention.1 = (bf16[256,640]{1,0:T(8,128)(2,1)S(1)}, bf16[256,640]{1,0:T(8,128)(2,1)S(1)}, bf16[256,640]{1,0:T(8,128)(2,1)S(1)}) custom-call(bf16[256,640]{1,0:T(8,128)(2,1)S(1)} %copy-done.1, bf16[256,640]{1,0:T(8,128)(2,1)S(1)} %copy-done.2, bf16[256,640]{1,0:T(8,128)(2,1)S(1)} %copy-done.3, bf16[256,640]{1,0:T(8,128)(2,1)S(1)} %copy-done.4, ...), custom_call_target="tpu_custom_call" | custom-call | tf_op jit(solution)/shard_map/attention/pallas_call | solution.py:276
  107.5 0.4 fusion.1
  107.9 38.4 %all-reduce.6 = (bf16[3,256,128]{1,2,0:T(8,128)(2,1)S(1)}, bf16[3,256,128]{1,2,0:T(8,128)(2,1)S(1)}) all-reduce(f32[3,256,128]{1,2,0:T(8,128)S(1)} %fusion.1, f32[3,256,128]{1,2,0:T(8,128)S(1)} %convolution_bitcast_fusion), channel_id=1, replica_groups=mesh['ctx'=16,'head'=8] {'head'}, use_global_device_ids=true, to_apply=%region_0.0 | all-reduce | flops 196608 | bytes 1179648 | tf_op jit(solution)/shard_map/psum | solution.py:335
  146.3 0.0 copy-start.9
  146.3 1.3 convolution_multiply_fusion
  147.6 0.0 copy-done.9
  147.6 1.3 fusion
  148.9 0.0 all-reduce.5.cloned.1.call-update
  148.9 149.2 %all-reduce.5.cloned.1.call-done = (f32[3,640,128]{1,2,0:T(8,128)}, f32[3,128,640]{2,1,0:T(8,128)}) async-done(((f32[3,640,128]{1,2,0:T(8,128)}, f32[3,128,640]{2,1,0:T(8,128)}), (f32[3,640,128]{1,2,0:T(8,128)}, f32[3,128,640]{2,1,0:T(8,128)})) %all-reduce.5.cloned.1.call-update) | async-done | bytes 1966096 | tf_op jit(solution)/shard_map/psum | solution.py:342
  298.1 2.5 copy.16
  300.6 0.7 copy.26
  301.3 0.7 copy.27
  302.1 0.7 copy.28
  302.8 0.9 copy.29
  (6 shorter events, 0.0 us)
Async XLA Ops:
  7.2 1.0 copy-start
  7.2 2.4 copy-start.8
  7.2 2.4 copy-start.7
  7.2 2.4 copy-start.6
  7.2 2.4 copy-start.3
  7.2 2.4 copy-start.2
  7.2 2.4 copy-start.1
  7.2 290.9 %all-reduce.5.cloned.1.call-start = ((), (), s32[]{:S(2)}) async-start(), calls=%async_computation | async-start | bytes 3932160 | tf_op jit(solution)/shard_map/psum | solution.py:342
  9.6 1.0 copy-start.4
  10.6 1.0 copy-start.5
  11.6 95.9 %copy-start.11 = (bf16[3,128,640]{2,1,0:T(8,128)(2,1)S(1)}, bf16[3,128,640]{2,1,0:T(8,128)(2,1)}, u32[]{:S(2)}) copy-start(bf16[3,128,640]{2,1,0:T(8,128)(2,1)} %param.19) | copy-start | bytes 1474564
  146.3 1.3 copy-start.9
  300.6 2.2 copy-start.10
Sparse Core Ops, SparseCore 0:
  149.0 149.0 all-reduce.4

commit v2 on v1

--- a/solution.py
+++ b/solution.py
@@ -21,6 +21,10 @@
 KEYS = SPAN * TOKENS
 TILE = 256
 WORKERS = HEADS * PARTS
+GROUPS = 8
+SHARE = TOKENS // GROUPS
+CHIPS = RING // 2
+BLOCKS = 3 * HEADS
 SCALE = WIDTH ** -0.5
 LOG2E = math.log2(math.e)
 DEAD = 1e30
@@ -39,16 +43,26 @@
     return pl.ds(pl.multiple_of(h * WIDTH, WIDTH), WIDTH)
 
 
-def attention_kernel(
-    q_ref, k_ref, v_ref, o_ref, g_ref, lse_ref, att_ref, used_ref,
-    qg_ref, kg_ref, vg_ref,
+def tn(a, b):
+    return lax.dot_general(a, b, (((0,), (0,)), ((), ())), preferred_element_type=F32)
+
+
+def layer_kernel(
+    q_ref, k_ref, v_ref, o_ref, g_ref, lse_ref, f_ref, down_ref, up_ref, att_ref, used_ref,
+    qg_ref, kg_ref, vg_ref, down_out, up_out,
     stats, rq, rg, rs, rk, rv, kt_buf, dk_acc, dv_acc, dq_acc,
     dqs, dks, dvs, rdq, rdk, rdv,
     q_send, g_send, s_send, k_send, v_send, dq_send, dk_send, dv_send,
     q_recv, g_recv, s_recv, k_recv, v_recv, dq_recv, dk_recv, dv_recv,
+    row_send, row_land, row_all, row_sems,
+    partial, pair_send, pair_land, sum_send, sum_land, total_all,
+    pair_sems, sum_sems, total_sems, twin_sems,
 ):
     me = lax.axis_index("ctx")
     group = lax.axis_index("head")
+    chip = me // 2
+    core = lax.rem(me, 2)
+    twin = me + 1 - 2 * core
 
     def move(src, dst, send_sem, recv_sem, target):
         return pltpu.make_async_remote_copy(
@@ -81,8 +95,62 @@
         )
         return carry
 
+    def greet_head(step, carry):
+        pl.semaphore_signal(
+            barrier, inc=1, device_id=(me, lax.rem(group + step, GROUPS)), device_id_type=MESH
+        )
+        return carry
+
     lax.fori_loop(1, RING, greet, 0)
-    pl.semaphore_wait(barrier, RING - 1)
+    lax.fori_loop(1, GROUPS, greet_head, 0)
+    pl.semaphore_wait(barrier, RING + GROUPS - 2)
+
+    def head_copy(kind, phase, other):
+        if phase == 0:
+            src, dst = row_send.at[kind, other], row_land.at[kind, group]
+        else:
+            src, dst = row_all.at[kind, group], row_all.at[kind, group]
+        return pltpu.make_async_remote_copy(
+            src_ref=src, dst_ref=dst,
+            send_sem=row_sems.at[kind, phase, 0, other],
+            recv_sem=row_sems.at[kind, phase, 1, group],
+            device_id=(me, other), device_id_type=MESH,
+        )
+
+    def to_heads(kind, phase):
+        def one(step, carry):
+            head_copy(kind, phase, lax.rem(group + step, GROUPS)).start()
+            return carry
+
+        lax.fori_loop(1, GROUPS, one, 0)
+
+    def from_heads(kind, phase):
+        def one(step, carry):
+            other = lax.rem(group + step, GROUPS)
+            dst = (row_land if phase == 0 else row_all).at[kind, other]
+            landed(dst, row_sems.at[kind, phase, 1, other])
+            return carry
+
+        lax.fori_loop(1, GROUPS, one, 0)
+
+    def drain_heads(kind, phase):
+        def one(step, carry):
+            head_copy(kind, phase, lax.rem(group + step, GROUPS)).wait_send()
+            return carry
+
+        lax.fori_loop(1, GROUPS, one, 0)
+
+    def split_rows(kind, m, rows):
+        row_send[kind, :, m] = rows.astype(BF16).reshape(GROUPS, SHARE, WIDTH)
+
+    def sum_rows(kind):
+        row_land[kind, group] = row_send[kind, group]
+        from_heads(kind, 0)
+        row_all[kind, group] = jnp.sum(row_land[kind].astype(F32), axis=0).astype(BF16)
+        to_heads(kind, 1)
+
+    def all_rows(kind, m):
+        return row_all[kind, :, m].reshape(TOKENS, WIDTH)
 
     my_part = me // SPAN
     my_place = lax.rem(me, SPAN)
@@ -146,6 +214,10 @@
 
     lax.fori_loop(0, RING, send_queries, 0)
 
+    for m in range(3):
+        split_rows(0, m, nn(f_ref[...], down_ref[m]))
+    to_heads(0, 0)
+
     my_head = me // PARTS
     work_part = lax.rem(me, PARTS)
 
@@ -159,6 +231,43 @@
             (dks.at[rows], rdk.at[my_head], dk_send.at[place], dk_recv.at[my_head], target),
             (dvs.at[rows], rdv.at[my_head], dv_send.at[place], dv_recv.at[my_head], target),
         )
+
+    def one_source(step, carry):
+        source = lax.rem(me - step + RING, RING)
+        landed(rs.at[source], s_recv.at[source])
+        landed(rq.at[source], q_recv.at[source])
+        landed(rg.at[source], g_recv.at[source])
+        queries = rq[source]
+        grads = rg[source]
+        norm = rs[source, 0:1, :]
+        row_dot = rs[source, 1:2, :]
+        code = rs[source, 2:3, :].astype(jnp.int32)
+        dq_acc[...] = jnp.zeros_like(dq_acc)
+
+        def one_tile(tile, inner):
+            rows = pl.ds(pl.multiple_of(tile * TILE, TILE), TILE)
+            keys = rk[rows]
+            scores = nt(keys, queries)
+            value_dot = nt(rv[rows], grads)
+            low_parts, grad_parts = [], []
+            for sub in range(TILE // 128):
+                bit = jnp.right_shift(code, tile * (TILE // 128) + sub) & 1
+                bias = jnp.where(bit > 0, norm, DEAD)
+                piece = slice(sub * 128, (sub + 1) * 128)
+                weights = jnp.exp2(scores[piece] * (SCALE * LOG2E) - bias)
+                low_parts.append(weights.astype(BF16))
+                grad_parts.append((weights * (value_dot[piece] - row_dot)).astype(BF16))
+            low = jnp.concatenate(low_parts, axis=0)
+            score_grad = jnp.concatenate(grad_parts, axis=0)
+            dv_acc[rows] += nn(low, grads)
+            dk_acc[rows] += nn(score_grad, queries)
+            dq_acc[...] += nn(kt_buf[:, rows], score_grad)
+            return inner
+
+        lax.fori_loop(0, KEYS // TILE, one_tile, 0, unroll=2)
+        dqs[source] = dq_acc[...].T.astype(BF16)
+        start(*dq_copy(source))
+        return carry
 
     @pl.when(me < WORKERS)
     def _work():
@@ -173,44 +282,13 @@
 
         lax.fori_loop(0, SPAN, keys_in, 0)
 
-        def one_source(step, carry):
-            source = lax.rem(me - step + RING, RING)
-            landed(rs.at[source], s_recv.at[source])
-            landed(rq.at[source], q_recv.at[source])
-            landed(rg.at[source], g_recv.at[source])
-            queries = rq[source]
-            grads = rg[source]
-            norm = rs[source, 0:1, :]
-            row_dot = rs[source, 1:2, :]
-            code = rs[source, 2:3, :].astype(jnp.int32)
-            dq_acc[...] = jnp.zeros_like(dq_acc)
-
-            def one_tile(tile, inner):
-                rows = pl.ds(pl.multiple_of(tile * TILE, TILE), TILE)
-                keys = rk[rows]
-                scores = nt(keys, queries)
-                value_dot = nt(rv[rows], grads)
-                low_parts, grad_parts = [], []
-                for sub in range(TILE // 128):
-                    bit = jnp.right_shift(code, tile * (TILE // 128) + sub) & 1
-                    bias = jnp.where(bit > 0, norm, DEAD)
-                    piece = slice(sub * 128, (sub + 1) * 128)
-                    weights = jnp.exp2(scores[piece] * (SCALE * LOG2E) - bias)
-                    low_parts.append(weights.astype(BF16))
-                    grad_parts.append((weights * (value_dot[piece] - row_dot)).astype(BF16))
-                low = jnp.concatenate(low_parts, axis=0)
-                score_grad = jnp.concatenate(grad_parts, axis=0)
-                dv_acc[rows] += nn(low, grads)
-                dk_acc[rows] += nn(score_grad, queries)
-                dq_acc[...] += nn(kt_buf[:, rows], score_grad)
-                return inner
-
-            lax.fori_loop(0, KEYS // TILE, one_tile, 0, unroll=2)
-            dqs[source] = dq_acc[...].T.astype(BF16)
-            start(*dq_copy(source))
-            return carry
-
-        lax.fori_loop(0, RING, one_source, 0)
+        lax.fori_loop(0, RING // 2, one_source, 0)
+
+    sum_rows(0)
+
+    @pl.when(me < WORKERS)
+    def _more_work():
+        lax.fori_loop(RING // 2, RING, one_source, 0)
 
         def keys_out(place, carry):
             rows = pl.ds(pl.multiple_of(place * TOKENS, TOKENS), TOKENS)
@@ -237,6 +315,110 @@
         kg_ref[:, columns] = rdk[h]
         landed(rdv.at[h], dv_recv.at[h])
         vg_ref[:, columns] = rdv[h]
+    from_heads(0, 1)
+
+    grads_out = (qg_ref, kg_ref, vg_ref)
+    for m in range(3):
+        split_rows(1, m, nt(grads_out[m][...], up_ref[m]))
+    to_heads(1, 0)
+
+    twin_copy = pltpu.make_async_remote_copy(
+        src_ref=pair_send, dst_ref=pair_land, send_sem=pair_sems.at[0], recv_sem=pair_sems.at[1],
+        device_id=(twin, group), device_id_type=MESH,
+    )
+
+    def chip_at(step):
+        return lax.rem(chip + step, CHIPS)
+
+    def sum_copy(other):
+        return pltpu.make_async_remote_copy(
+            src_ref=sum_send.at[other], dst_ref=sum_land.at[chip],
+            send_sem=sum_sems.at[0, other], recv_sem=sum_sems.at[1, chip],
+            device_id=(2 * other + core, group), device_id_type=MESH,
+        )
+
+    def total_copy(other):
+        return pltpu.make_async_remote_copy(
+            src_ref=total_all.at[core, chip], dst_ref=total_all.at[core, chip],
+            send_sem=total_sems.at[0, other], recv_sem=total_sems.at[1, chip],
+            device_id=(2 * other + core, group), device_id_type=MESH,
+        )
+
+    def pass_copy(origin):
+        return pltpu.make_async_remote_copy(
+            src_ref=total_all.at[core, origin], dst_ref=total_all.at[core, origin],
+            send_sem=twin_sems.at[0, origin], recv_sem=twin_sems.at[1, origin],
+            device_id=(twin, group), device_id_type=MESH,
+        )
+
+    def hand_over():
+        for block in range(BLOCKS):
+            pair_send[block] = partial[block].astype(BF16)
+        twin_copy.start()
+
+    def take_over():
+        twin_copy.wait_recv()
+        for block in range(BLOCKS):
+            both = partial[block] + pair_land[block].astype(F32)
+            sum_send[block // 2, block % 2] = both.astype(BF16)
+        sum_send[CHIPS - 1, 1] = jnp.zeros((WIDTH, WIDTH), BF16)
+        for step in range(1, CHIPS):
+            sum_copy(chip_at(step)).start()
+        sum_land[chip] = sum_send[chip]
+
+    for m in range(3):
+        rows = tn(all_rows(0, m), grads_out[m][...]) * adapter_scale
+        for h in range(HEADS):
+            partial[m * HEADS + h] = rows[:, h * WIDTH : (h + 1) * WIDTH]
+    pl.when(core == 1)(hand_over)
+    sum_rows(1)
+    pl.when(core == 0)(take_over)
+    from_heads(1, 1)
+
+    @pl.when(core == 0)
+    def _down_over():
+        for m in range(3):
+            rows = tn(f_ref[...], all_rows(1, m)) * adapter_scale
+            for h in range(HEADS):
+                pair_send[m * HEADS + h] = rows[h * WIDTH : (h + 1) * WIDTH].astype(BF16)
+        twin_copy.start()
+
+    @pl.when(core == 1)
+    def _down_sum():
+        for m in range(3):
+            rows = tn(f_ref[...], all_rows(1, m)) * adapter_scale
+            for h in range(HEADS):
+                partial[m * HEADS + h] = rows[h * WIDTH : (h + 1) * WIDTH]
+        take_over()
+
+    for step in range(1, CHIPS):
+        other = chip_at(step)
+        landed(sum_land.at[other], sum_sems.at[1, other])
+    total_all[core, chip] = jnp.sum(sum_land[...].astype(F32), axis=0).astype(BF16)
+    for step in range(1, CHIPS):
+        total_copy(chip_at(step)).start()
+    pass_copy(chip).start()
+    for step in range(1, CHIPS):
+        other = chip_at(step)
+        landed(total_all.at[core, other], total_sems.at[1, other])
+        pass_copy(other).start()
+    for origin in range(CHIPS):
+        landed(total_all.at[1 - core, origin], twin_sems.at[1, origin])
+    for block in range(BLOCKS):
+        m, h = block // HEADS, block % HEADS
+        columns = slice(h * WIDTH, (h + 1) * WIDTH)
+        up_out[m, :, columns] = total_all[0, block // 2, block % 2].astype(F32)
+        down_out[m, columns, :] = total_all[1, block // 2, block % 2].astype(F32)
+
+    for kind in range(2):
+        for phase in range(2):
+            drain_heads(kind, phase)
+    twin_copy.wait_send()
+    for step in range(1, CHIPS):
+        sum_copy(chip_at(step)).wait_send()
+        total_copy(chip_at(step)).wait_send()
+    for origin in range(CHIPS):
+        pass_copy(origin).wait_send()
 
     def drain_kv(h, carry):
         for copy in kv_copies(h):
@@ -268,16 +450,30 @@
         lax.fori_loop(0, SPAN, drain_keys, 0)
 
 
-def attention(queries, keys, values, output, grads, norm, blocks, used):
+def on_device(
+    queries,
+    key_matrix_rows,
+    value_matrix_rows,
+    attention_output,
+    output_gradient,
+    log_sum_norm,
+    features,
+    adapter_down_weight,
+    adapter_up_weight,
+    attended_key_blocks,
+    used_block_count,
+):
     vmem = pl.BlockSpec(memory_space=pltpu.VMEM)
     smem = pl.BlockSpec(memory_space=pltpu.SMEM)
     rows = jax.ShapeDtypeStruct((TOKENS, HEADS * WIDTH), BF16)
+    down = jax.ShapeDtypeStruct((3, HEADS * WIDTH, WIDTH), F32)
+    up = jax.ShapeDtypeStruct((3, WIDTH, HEADS * WIDTH), F32)
     dma = pltpu.SemaphoreType.DMA
     return pl.pallas_call(
-        attention_kernel,
-        out_shape=(rows, rows, rows),
-        in_specs=[vmem] * 6 + [smem] * 2,
-        out_specs=(vmem, vmem, vmem),
+        layer_kernel,
+        out_shape=(rows, rows, rows, down, up),
+        in_specs=[vmem] * 9 + [smem] * 2,
+        out_specs=(vmem,) * 5,
         scratch_shapes=[
             pltpu.VMEM((WORKERS, 8, TOKENS), F32),
             pltpu.VMEM((RING, TOKENS, WIDTH), BF16),
@@ -299,48 +495,27 @@
             dma((RING,)), dma((SPAN,)), dma((SPAN,)),
             dma((RING,)), dma((RING,)), dma((RING,)), dma((SPAN,)), dma((SPAN,)),
             dma((WORKERS,)), dma((HEADS,)), dma((HEADS,)),
+            pltpu.VMEM((2, GROUPS, 3, SHARE, WIDTH), BF16),
+            pltpu.VMEM((2, GROUPS, 3, SHARE, WIDTH), BF16),
+            pltpu.VMEM((2, GROUPS, 3, SHARE, WIDTH), BF16),
+            dma((2, 2, 2, GROUPS)),
+            pltpu.VMEM((BLOCKS, WIDTH, WIDTH), F32),
+            pltpu.VMEM((BLOCKS, WIDTH, WIDTH), BF16),
+            pltpu.VMEM((BLOCKS, WIDTH, WIDTH), BF16),
+            pltpu.VMEM((CHIPS, 2, WIDTH, WIDTH), BF16),
+            pltpu.VMEM((CHIPS, 2, WIDTH, WIDTH), BF16),
+            pltpu.VMEM((2, CHIPS, 2, WIDTH, WIDTH), BF16),
+            dma((2,)), dma((2, CHIPS)), dma((2, CHIPS)), dma((2, CHIPS)),
         ],
         compiler_params=pltpu.CompilerParams(
             collective_id=0, has_side_effects=True, vmem_limit_bytes=48 * 2**20
         ),
-        name="attention",
-    )(queries, keys, values, output, grads, norm, blocks, used)
-
-
-def on_device(
-    queries,
-    key_matrix_rows,
-    value_matrix_rows,
-    attention_output,
-    output_gradient,
-    log_sum_norm,
-    features,
-    adapter_down_weight,
-    adapter_up_weight,
-    attended_key_blocks,
-    used_block_count,
-):
-    down_piece = jnp.einsum(
-        "vc,fco->fvo", features, adapter_down_weight, preferred_element_type=jnp.float32
+        name="layer",
+    )(
+        queries, key_matrix_rows, value_matrix_rows, attention_output, output_gradient,
+        log_sum_norm, features, adapter_down_weight, adapter_up_weight,
+        attended_key_blocks, used_block_count,
     )
-    projected_rows = lax.psum(down_piece, "head").astype(jnp.bfloat16)
-    query_grad, key_grad, value_grad = attention(
-        queries, key_matrix_rows, value_matrix_rows, attention_output, output_gradient,
-        log_sum_norm, attended_key_blocks, used_block_count,
-    )
-    shifted_rows = jnp.stack([query_grad, key_grad, value_grad])
-    head_piece = jnp.einsum(
-        "oki,oji->okj", shifted_rows, adapter_up_weight, preferred_element_type=jnp.float32
-    )
-    collected_rows = lax.psum(head_piece, "head").astype(jnp.bfloat16)
-    up_piece = adapter_scale * jnp.einsum(
-        "pjf,pjd->pfd", projected_rows, shifted_rows, preferred_element_type=jnp.float32
-    )
-    down_piece_gradient = adapter_scale * jnp.einsum(
-        "sq,ysw->yqw", features, collected_rows, preferred_element_type=jnp.float32
-    )
-    down_matrix_gradient, up_matrix_gradient = lax.psum((down_piece_gradient, up_piece), "ctx")
-    return (query_grad, key_grad, value_grad, down_matrix_gradient, up_matrix_gradient)
 
 
 def solution(mesh):

time: 311 us -> 147 us (0.47)
  waiting for transfers between devices: 149 us -> 0 us
  blocking collectives: 38.4 us -> 0 us
  Pallas kernels: 95.9 us -> 131 us
  between operations: 14.2 us -> 0.66 us
  local copies, waits for them, and re-layouts: 8.5 us -> 14 us
  matrix products: 4.33 us -> 0 us
    psum x1 -> x0, waiting for transfers between devices: 149 us -> none  [on_device(): lax.psum((down_piece_gradient, up_piece), 'ctx')]
    psum x1 -> x0, blocking collectives: 38.4 us -> none  [on_device(): collected_rows = lax.psum(head_piece, 'head').astype(jnp.bfloat16)]
    pallas_call x1, Pallas kernels: 95.9 us -> 131 us  [on_device(): pl.pallas_call(layer_kernel, out_shape=(rows, rows, rows, down, up), in_s...]
    unnamed x29 -> x27, local copies, waits for them, and re-layouts: 8.5 us -> 14 us
    dot_general x4 -> x0, matrix products: 4.33 us -> none  [the longest x1 1.33 us: on_device(): jnp.einsum('vc,fco->fvo', features, adapter_down_weight, preferred_elemen...]
  transfers between devices with their start and end apart: 1 -> 0, of which waited for: 1 -> 0; matrix products, arithmetic and copies ran while one was open for 0% -> 0% of each run, Pallas kernels for 0% -> 0%
where the time goes in v2:
time: 147 us; the launch traced here: 146 us
  Pallas kernels  131 us (89%)
  local copies, waits for them, and re-layouts  14 us (10%)
    pallas_call x1, Pallas kernels, on_device(): pl.pallas_call(layer_kernel, out_shape=(rows, rows, rows, down, up), in_s...  131 us
    unnamed x27, local copies, waits for them, and re-layouts  14 us

profile of v2, /device:TPU:1, one launch (start us, length us, event | category | flops | bytes accessed | tf_op | source)
XLA Modules:
  0.0 146.1 jit_solution(14056964502765672579)
XLA Ops:
  0.6 0.0 copy-start
  0.6 1.0 copy-done
  1.7 0.0 copy-start.1
  1.7 1.0 copy-done.1
  2.7 0.0 copy-start.2
  2.7 1.0 copy-done.2
  3.7 0.0 copy-start.3
  3.7 1.0 copy-done.3
  4.6 0.0 copy-start.4
  4.6 1.0 copy-done.4
  5.6 0.0 copy-start.5
  5.6 1.0 copy-done.5
  6.6 0.0 copy-start.6
  6.6 1.0 copy-done.6
  7.6 0.0 copy-start.7
  7.6 1.0 copy-done.7
  8.5 0.0 copy-start.8
  8.5 0.7 copy-done.8
  9.2 0.0 copy-start.9
  9.2 0.7 copy-done.9
  9.9 0.0 copy-start.10
  9.9 0.7 copy-done.10
  10.6 131.5 %layer.1 = (bf16[256,640]{1,0:T(8,128)(2,1)S(1)}, bf16[256,640]{1,0:T(8,128)(2,1)S(1)}, bf16[256,640]{1,0:T(8,128)(2,1)S(1)}, f32[3,640,128]{2,1,0:T(8,128)S(1)}, f32[3,128,640]{2,1,0:T(8,128)S(1)}) custom-call(bf16[256,640]{1,0:T(8,128)(2,1)S(1)} %copy-done.2, bf16[256,640]{1,0:T(8,128)(2,1)S(1)} %copy-done.3, bf16[256,640]{1,0:T(8,128)(2,1)S(1)} %copy-done.4, ...), custom_call_target="tpu_custom_call" | custom-call | tf_op jit(solution)/shard_map/layer/pallas_call | solution.py:472
  142.0 0.7 copy.21
  142.8 0.7 copy.22
  143.5 0.7 copy.23
  144.2 0.9 copy.24
  145.2 0.9 copy.25
Async XLA Ops:
  0.6 1.0 copy-start
  1.7 1.0 copy-start.1
  2.7 1.0 copy-start.2
  3.7 1.0 copy-start.3
  4.6 1.0 copy-start.4
  5.6 1.0 copy-start.5
  6.6 1.0 copy-start.6
  7.6 1.0 copy-start.7
  8.5 0.7 copy-start.8
  9.2 0.7 copy-start.9
  9.9 0.7 copy-start.10

commit v3 on v2

v3 whole, which is shorter than its diff:
```python
import functools
import math

import jax
import jax.numpy as jnp
from jax import lax
from jax.experimental import pallas as pl
from jax.experimental.pallas import tpu as pltpu
from jax.sharding import PartitionSpec as P

MESH = pl.DeviceIdType.MESH
BF16 = jnp.bfloat16
F32 = jnp.float32

HEADS = 5
WIDTH = 128
TOKENS = 256
RING = 16
BLOCK = 128
GROUPS = 8
SHARE = TOKENS // GROUPS
CHIPS = RING // 2
BLOCKS = 3 * HEADS
SCALE = WIDTH ** -0.5
LOG2E = math.log2(math.e)
DEAD = 1e30
adapter_scale = 0.125


def nt(a, b):
    return lax.dot_general(a, b, (((1,), (1,)), ((), ())), preferred_element_type=F32)


def nn(a, b):
    return lax.dot_general(a, b, (((1,), (0,)), ((), ())), preferred_element_type=F32)


def lane_slice(h):
    return pl.ds(pl.multiple_of(h * WIDTH, WIDTH), WIDTH)


def tn(a, b):
    return lax.dot_general(a, b, (((0,), (0,)), ((), ())), preferred_element_type=F32)


def layer_kernel(
    q_ref, k_ref, v_ref, o_ref, g_ref, lse_ref, f_ref, down_ref, up_ref, att_ref, used_ref,
    qg_ref, kg_ref, vg_ref, down_out, up_out,
    o_here, g_here, lse_here, f_here, down_here, up_here, in_sems,
    stats, rs, rqg, rkv, keys_t, dk_acc, dv_acc, dq_acc, dq_land, dq_out, dkv_out, rdq, rdkv,
    s_send, qg_send, kv_send, pass_send, dq_pair_send, dq_send, dkv_send,
    s_recv, qg_recv, kv_recv, pass_recv, dq_pair_recv, dq_recv, dkv_recv,
    row_send, row_land, row_all, row_sems,
    partial, pair_send, pair_land, sum_send, sum_land, total_all,
    pair_sems, sum_sems, total_sems, twin_sems,
):
    me = lax.axis_index("ctx")
    group = lax.axis_index("head")
    chip = me // 2
    core = lax.rem(me, 2)
    twin = me + 1 - 2 * core

    def chip_at(step):
        return lax.rem(chip + step, CHIPS)

    def move(src, dst, send_sem, recv_sem, target):
        return pltpu.make_async_remote_copy(
            src_ref=src, dst_ref=dst, send_sem=send_sem, recv_sem=recv_sem,
            device_id=(target, group), device_id_type=MESH,
        )

    def start(src, dst, send_sem, recv_sem, target):
        @pl.when(target != me)
        def _():
            move(src, dst, send_sem, recv_sem, target).start()

        @pl.when(target == me)
        def _():
            pltpu.make_async_copy(src, dst, recv_sem).start()

    def sent(src, dst, send_sem, recv_sem, target):
        @pl.when(target != me)
        def _():
            move(src, dst, send_sem, recv_sem, target).wait_send()

    def landed(dst, recv_sem):
        pltpu.make_async_copy(dst, dst, recv_sem).wait()

    barrier = pltpu.get_barrier_semaphore()

    def greet(step, carry):
        pl.semaphore_signal(
            barrier, inc=1, device_id=(2 * chip_at(step) + core, group), device_id_type=MESH
        )
        return carry

    def greet_head(step, carry):
        pl.semaphore_signal(
            barrier, inc=1, device_id=(me, lax.rem(group + step, GROUPS)), device_id_type=MESH
        )
        return carry

    pl.semaphore_signal(barrier, inc=1, device_id=(twin, group), device_id_type=MESH)
    lax.fori_loop(1, CHIPS, greet, 0)
    lax.fori_loop(1, GROUPS, greet_head, 0)

    inputs = [
        pltpu.make_async_copy(src, dst, in_sems.at[index])
        for index, (src, dst) in enumerate(
            (
                (g_ref, g_here), (o_ref, o_here), (lse_ref, lse_here),
                (f_ref, f_here), (down_ref, down_here), (up_ref, up_here),
            )
        )
    ]
    for copy in inputs:
        copy.start()

    lane = lax.broadcasted_iota(jnp.int32, (1, TOKENS), 1)
    words = [[jnp.int32(0), jnp.int32(0)], [jnp.int32(0), jnp.int32(0)]]
    for row in range(2):
        for slot in range(16):
            block = att_ref[row, slot]
            owner = jnp.right_shift(block, 1)
            bit = jnp.left_shift(jnp.int32(1), jnp.right_shift(block, 2) * 2 + (block & 1))
            for part in range(2):
                inside = ((owner & 1) == part) & (slot < used_ref[row])
                words[part][row] = words[part][row] | jnp.where(inside, bit, 0)
    codes = [
        jnp.where(lane < TOKENS // 2, word[0], word[1]).astype(F32) for word in words
    ]
    for copy in inputs[:3]:
        copy.wait()
    for h in range(HEADS):
        columns = slice(h * WIDTH, (h + 1) * WIDTH)
        product = g_here[:, columns].astype(F32) * o_here[:, columns].astype(F32)
        row_dot = jnp.sum(product.T, axis=0, keepdims=True)
        norm = lse_here[h : h + 1, :] * LOG2E
        stats[h] = jnp.concatenate(
            [norm, row_dot, codes[0], codes[1], jnp.zeros((4, TOKENS), F32)], axis=0
        )

    pl.semaphore_wait(barrier, CHIPS + GROUPS - 1)

    def query_copies(h):
        target = 2 * lax.rem(5 * h, CHIPS) + core
        lanes = lane_slice(h)
        return (
            (stats.at[h], rs.at[chip, core], s_send.at[h], s_recv.at[chip], target),
            (q_ref.at[:, lanes], rqg.at[chip, core, 0], qg_send.at[0, h], qg_recv.at[chip], target),
            (g_ref.at[:, lanes], rqg.at[chip, core, 1], qg_send.at[1, h], qg_recv.at[chip], target),
        )

    def key_copies(h):
        target = 2 * lax.rem(5 * h, CHIPS) + core
        lanes = lane_slice(h)
        return (
            (k_ref.at[:, lanes], rkv.at[chip, 0], kv_send.at[0, h], kv_recv.at[chip], target),
            (v_ref.at[:, lanes], rkv.at[chip, 1], kv_send.at[1, h], kv_recv.at[chip], target),
        )

    def send_all(copies):
        def one(step, carry):
            h = lax.rem(5 * lax.rem(chip - step + CHIPS, CHIPS), CHIPS)

            @pl.when(h < HEADS)
            def _():
                for copy in copies(h):
                    start(*copy)

            return carry

        lax.fori_loop(0, CHIPS, one, 0)

    send_all(query_copies)
    send_all(key_copies)

    def head_copy(kind, phase, other):
        if phase == 0:
            src, dst = row_send.at[kind, other], row_land.at[kind, group]
        else:
            src, dst = row_all.at[kind, group], row_all.at[kind, group]
        return pltpu.make_async_remote_copy(
            src_ref=src, dst_ref=dst,
            send_sem=row_sems.at[kind, phase, 0, other],
            recv_sem=row_sems.at[kind, phase, 1, group],
            device_id=(me, other), device_id_type=MESH,
        )

    def to_heads(kind, phase):
        def one(step, carry):
            head_copy(kind, phase, lax.rem(group + step, GROUPS)).start()
            return carry

        lax.fori_loop(1, GROUPS, one, 0)

    def from_heads(kind, phase):
        def one(step, carry):
            other = lax.rem(group + step, GROUPS)
            dst = (row_land if phase == 0 else row_all).at[kind, other]
            landed(dst, row_sems.at[kind, phase, 1, other])
            return carry

        lax.fori_loop(1, GROUPS, one, 0)

    def drain_heads(kind, phase):
        def one(step, carry):
            head_copy(kind, phase, lax.rem(group + step, GROUPS)).wait_send()
            return carry

        lax.fori_loop(1, GROUPS, one, 0)

    def split_rows(kind, m, rows):
        row_send[kind, :, m] = rows.astype(BF16).reshape(GROUPS, SHARE, WIDTH)

    def sum_rows(kind):
        row_land[kind, group] = row_send[kind, group]
        from_heads(kind, 0)
        row_all[kind, group] = jnp.sum(row_land[kind].astype(F32), axis=0).astype(BF16)
        to_heads(kind, 1)

    def all_rows(kind, m):
        return row_all[kind, :, m].reshape(TOKENS, WIDTH)

    inputs[3].wait()
    inputs[4].wait()
    for m in range(3):
        split_rows(0, m, nn(f_here[...], down_here[m]))
    to_heads(0, 0)

    my_head = lax.rem(5 * chip, CHIPS)
    working = my_head < HEADS

    def pass_copies(origin):
        return (
            (rs.at[origin, core], rs.at[origin, core],
             pass_send.at[0, origin], pass_recv.at[0, origin], twin),
            (rqg.at[origin, core], rqg.at[origin, core],
             pass_send.at[1, origin], pass_recv.at[1, origin], twin),
        )

    def dq_pair_copy(origin):
        return (dq_acc.at[origin, 1 - core], dq_land.at[origin],
                dq_pair_send.at[origin], dq_pair_recv.at[origin], twin)

    def dq_copy(origin):
        return (dq_out.at[origin], rdq.at[my_head],
                dq_send.at[origin], dq_recv.at[my_head], 2 * origin + core)

    def dkv_copy(origin):
        return (dkv_out.at[origin], rdkv.at[my_head],
                dkv_send.at[origin], dkv_recv.at[my_head], 2 * origin + core)

    def compute(key_chip, origin, first):
        keys = rkv[key_chip, 0]
        queries = rqg[origin, :, 0].reshape(2 * TOKENS, WIDTH)
        grads = rqg[origin, :, 1].reshape(2 * TOKENS, WIDTH)
        norm = jnp.concatenate([rs[origin, side, 0:1, :] for side in range(2)], axis=1)
        row_dot = jnp.concatenate([rs[origin, side, 1:2, :] for side in range(2)], axis=1)
        code = jnp.concatenate(
            [
                jnp.where(core == 0, rs[origin, side, 2:3, :], rs[origin, side, 3:4, :])
                for side in range(2)
            ],
            axis=1,
        ).astype(jnp.int32)
        scores = nt(keys, queries)
        value_dot = nt(rkv[key_chip, 1], grads)
        low_parts, grad_parts = [], []
        for sub in range(2):
            bit = jnp.right_shift(code, key_chip * 2 + sub) & 1
            bias = jnp.where(bit > 0, norm, DEAD)
            piece = slice(sub * BLOCK, (sub + 1) * BLOCK)
            weights = jnp.exp2(scores[piece] * (SCALE * LOG2E) - bias)
            low_parts.append(weights.astype(BF16))
            grad_parts.append(
                (weights * ((value_dot[piece] - row_dot) * SCALE)).astype(BF16)
            )
        low = jnp.concatenate(low_parts, axis=0)
        score_grad = jnp.concatenate(grad_parts, axis=0)
        dv_acc[...] += nn(low, grads)
        dk_acc[...] += nn(score_grad, queries)
        dq_part = nn(keys_t[...], score_grad)
        for side in range(2):
            piece = dq_part[:, side * TOKENS : (side + 1) * TOKENS]
            if first:
                dq_acc[origin, side] = piece
            else:
                dq_acc[origin, side] += piece

    def open_keys(key_chip):
        landed(rkv.at[key_chip], kv_recv.at[key_chip])
        keys_t[...] = rkv[key_chip, 0].astype(F32).T.astype(BF16)
        dk_acc[...] = jnp.zeros_like(dk_acc)
        dv_acc[...] = jnp.zeros_like(dv_acc)

    def close_keys(key_chip):
        dkv_out[key_chip, 0] = dk_acc[...].astype(BF16)
        dkv_out[key_chip, 1] = dv_acc[...].astype(BF16)
        start(*dkv_copy(key_chip))

    @pl.when(working)
    def _first_keys():
        open_keys(chip)

        def receive(step, carry):
            origin = chip_at(step)
            landed(rs.at[origin, core], s_recv.at[origin])
            landed(rqg.at[origin, core], qg_recv.at[origin])
            for copy in pass_copies(origin):
                move(*copy).start()
            return carry

        def use(step, carry):
            origin = chip_at(step)
            landed(rs.at[origin, 1 - core], pass_recv.at[0, origin])
            landed(rqg.at[origin, 1 - core], pass_recv.at[1, origin])
            compute(chip, origin, True)
            return carry

        receive(0, 0)

        def both(step, carry):
            receive(step, carry)
            return use(step - 1, carry)

        lax.fori_loop(1, CHIPS, both, 0)
        use(CHIPS - 1, 0)
        close_keys(chip)

    sum_rows(0)

    @pl.when(working)
    def _other_keys():
        def middle(turn, carry):
            key_chip = chip_at(turn)
            open_keys(key_chip)

            def one(step, inner):
                compute(key_chip, chip_at(step), False)
                return inner

            lax.fori_loop(0, CHIPS, one, 0)
            close_keys(key_chip)
            return carry

        lax.fori_loop(1, CHIPS - 1, middle, 0)

        key_chip = chip_at(CHIPS - 1)
        open_keys(key_chip)

        def finish(step):
            origin = chip_at(step)
            landed(dq_land.at[origin], dq_pair_recv.at[origin])
            total = dq_acc[origin, core] + dq_land[origin]
            dq_out[origin] = total.T.astype(BF16)
            start(*dq_copy(origin))

        def last(step, carry):
            origin = chip_at(step)
            compute(key_chip, origin, False)
            move(*dq_pair_copy(origin)).start()

            @pl.when(step > 0)
            def _():
                finish(step - 1)

            return carry

        lax.fori_loop(0, CHIPS, last, 0)
        close_keys(key_chip)
        finish(CHIPS - 1)

    for h in range(HEADS):
        columns = slice(h * WIDTH, (h + 1) * WIDTH)
        landed(rdkv.at[h], dkv_recv.at[h])
        kg_ref[:, columns] = rdkv[h, 0]
        vg_ref[:, columns] = rdkv[h, 1]
    from_heads(0, 1)
    inputs[5].wait()

    grads_out = (qg_ref, kg_ref, vg_ref)

    def gather_rows(m):
        split_rows(1, m, nt(grads_out[m][...], up_here[m]))

    def up_rows(m):
        rows = tn(all_rows(0, m), grads_out[m][...]) * adapter_scale
        for h in range(HEADS):
            partial[m * HEADS + h] = rows[:, h * WIDTH : (h + 1) * WIDTH]

    for m in (1, 2):
        gather_rows(m)
        up_rows(m)
    for h in range(HEADS):
        landed(rdq.at[h], dq_recv.at[h])
        qg_ref[:, h * WIDTH : (h + 1) * WIDTH] = rdq[h]
    gather_rows(0)
    to_heads(1, 0)
    up_rows(0)

    twin_copy = pltpu.make_async_remote_copy(
        src_ref=pair_send, dst_ref=pair_land, send_sem=pair_sems.at[0], recv_sem=pair_sems.at[1],
        device_id=(twin, group), device_id_type=MESH,
    )

    def sum_copy(other):
        return pltpu.make_async_remote_copy(
            src_ref=sum_send.at[other], dst_ref=sum_land.at[chip],
            send_sem=sum_sems.at[0, other], recv_sem=sum_sems.at[1, chip],
            device_id=(2 * other + core, group), device_id_type=MESH,
        )

    def total_copy(other):
        return pltpu.make_async_remote_copy(
            src_ref=total_all.at[core, chip], dst_ref=total_all.at[core, chip],
            send_sem=total_sems.at[0, other], recv_sem=total_sems.at[1, chip],
            device_id=(2 * other + core, group), device_id_type=MESH,
        )

    def pass_copy(origin):
        return pltpu.make_async_remote_copy(
            src_ref=total_all.at[core, origin], dst_ref=total_all.at[core, origin],
            send_sem=twin_sems.at[0, origin], recv_sem=twin_sems.at[1, origin],
            device_id=(twin, group), device_id_type=MESH,
        )

    def hand_over():
        for block in range(BLOCKS):
            pair_send[block] = partial[block].astype(BF16)
        twin_copy.start()

    def take_over():
        twin_copy.wait_recv()
        for block in range(BLOCKS):
            both = partial[block] + pair_land[block].astype(F32)
            sum_send[block // 2, block % 2] = both.astype(BF16)
        sum_send[CHIPS - 1, 1] = jnp.zeros((WIDTH, WIDTH), BF16)
        for step in range(1, CHIPS):
            sum_copy(chip_at(step)).start()
        sum_land[chip] = sum_send[chip]

    pl.when(core == 1)(hand_over)
    sum_rows(1)
    pl.when(core == 0)(take_over)
    from_heads(1, 1)

    @pl.when(core == 0)
    def _down_over():
        for m in range(3):
            rows = tn(f_here[...], all_rows(1, m)) * adapter_scale
            for h in range(HEADS):
                pair_send[m * HEADS + h] = rows[h * WIDTH : (h + 1) * WIDTH].astype(BF16)
        twin_copy.start()

    @pl.when(core == 1)
    def _down_sum():
        for m in range(3):
            rows = tn(f_here[...], all_rows(1, m)) * adapter_scale
            for h in range(HEADS):
                partial[m * HEADS + h] = rows[h * WIDTH : (h + 1) * WIDTH]
        take_over()

    for step in range(1, CHIPS):
        other = chip_at(step)
        landed(sum_land.at[other], sum_sems.at[1, other])
    total_all[core, chip] = jnp.sum(sum_land[...].astype(F32), axis=0).astype(BF16)
    for step in range(1, CHIPS):
        total_copy(chip_at(step)).start()
    pass_copy(chip).start()
    for step in range(1, CHIPS):
        other = chip_at(step)
        landed(total_all.at[core, other], total_sems.at[1, other])
        pass_copy(other).start()
    for origin in range(CHIPS):
        landed(total_all.at[1 - core, origin], twin_sems.at[1, origin])
    for block in range(BLOCKS):
        m, h = block // HEADS, block % HEADS
        columns = slice(h * WIDTH, (h + 1) * WIDTH)
        up_out[m, :, columns] = total_all[0, block // 2, block % 2].astype(F32)
        down_out[m, columns, :] = total_all[1, block // 2, block % 2].astype(F32)

    for kind in range(2):
        for phase in range(2):
            drain_heads(kind, phase)
    twin_copy.wait_send()
    for step in range(1, CHIPS):
        sum_copy(chip_at(step)).wait_send()
        total_copy(chip_at(step)).wait_send()
    for origin in range(CHIPS):
        pass_copy(origin).wait_send()

    def drain_sends(h, carry):
        for copy in query_copies(h) + key_copies(h):
            sent(*copy)
        return carry

    lax.fori_loop(0, HEADS, drain_sends, 0)

    @pl.when(working)
    def _drain_work():
        def one(origin, carry):
            for copy in pass_copies(origin) + (dq_pair_copy(origin),):
                move(*copy).wait_send()
            sent(*dq_copy(origin))
            sent(*dkv_copy(origin))
            return carry

        lax.fori_loop(0, CHIPS, one, 0)


def on_device(
    queries,
    key_matrix_rows,
    value_matrix_rows,
    attention_output,
    output_gradient,
    log_sum_norm,
    features,
    adapter_down_weight,
    adapter_up_weight,
    attended_key_blocks,
    used_block_count,
):
    vmem = pl.BlockSpec(memory_space=pltpu.VMEM)
    smem = pl.BlockSpec(memory_space=pltpu.SMEM)
    rows = jax.ShapeDtypeStruct((TOKENS, HEADS * WIDTH), BF16)
    down = jax.ShapeDtypeStruct((3, HEADS * WIDTH, WIDTH), F32)
    up = jax.ShapeDtypeStruct((3, WIDTH, HEADS * WIDTH), F32)
    dma = pltpu.SemaphoreType.DMA
    return pl.pallas_call(
        layer_kernel,
        out_shape=(rows, rows, rows, down, up),
        in_specs=[pl.BlockSpec(memory_space=pl.ANY)] * 9 + [smem] * 2,
        out_specs=(vmem,) * 5,
        scratch_shapes=[
            pltpu.VMEM((TOKENS, HEADS * WIDTH), BF16),
            pltpu.VMEM((TOKENS, HEADS * WIDTH), BF16),
            pltpu.VMEM((HEADS, TOKENS), F32),
            pltpu.VMEM((TOKENS, HEADS * WIDTH), BF16),
            pltpu.VMEM((3, HEADS * WIDTH, WIDTH), BF16),
            pltpu.VMEM((3, WIDTH, HEADS * WIDTH), BF16),
            dma((6,)),
            pltpu.VMEM((HEADS, 8, TOKENS), F32),
            pltpu.VMEM((CHIPS, 2, 8, TOKENS), F32),
            pltpu.VMEM((CHIPS, 2, 2, TOKENS, WIDTH), BF16),
            pltpu.VMEM((CHIPS, 2, TOKENS, WIDTH), BF16),
            pltpu.VMEM((WIDTH, TOKENS), BF16),
            pltpu.VMEM((TOKENS, WIDTH), F32),
            pltpu.VMEM((TOKENS, WIDTH), F32),
            pltpu.VMEM((CHIPS, 2, WIDTH, TOKENS), F32),
            pltpu.VMEM((CHIPS, WIDTH, TOKENS), F32),
            pltpu.VMEM((CHIPS, TOKENS, WIDTH), BF16),
            pltpu.VMEM((CHIPS, 2, TOKENS, WIDTH), BF16),
            pltpu.VMEM((HEADS, TOKENS, WIDTH), BF16),
            pltpu.VMEM((HEADS, 2, TOKENS, WIDTH), BF16),
            dma((HEADS,)), dma((2, HEADS)), dma((2, HEADS)), dma((2, CHIPS)),
            dma((CHIPS,)), dma((CHIPS,)), dma((CHIPS,)),
            dma((CHIPS,)), dma((CHIPS,)), dma((CHIPS,)), dma((2, CHIPS)),
            dma((CHIPS,)), dma((HEADS,)), dma((HEADS,)),
            pltpu.VMEM((2, GROUPS, 3, SHARE, WIDTH), BF16),
            pltpu.VMEM((2, GROUPS, 3, SHARE, WIDTH), BF16),
            pltpu.VMEM((2, GROUPS, 3, SHARE, WIDTH), BF16),
            dma((2, 2, 2, GROUPS)),
            pltpu.VMEM((BLOCKS, WIDTH, WIDTH), F32),
            pltpu.VMEM((BLOCKS, WIDTH, WIDTH), BF16),
            pltpu.VMEM((BLOCKS, WIDTH, WIDTH), BF16),
            pltpu.VMEM((CHIPS, 2, WIDTH, WIDTH), BF16),
            pltpu.VMEM((CHIPS, 2, WIDTH, WIDTH), BF16),
            pltpu.VMEM((2, CHIPS, 2, WIDTH, WIDTH), BF16),
            dma((2,)), dma((2, CHIPS)), dma((2, CHIPS)), dma((2, CHIPS)),
        ],
        compiler_params=pltpu.CompilerParams(
            collective_id=0, has_side_effects=True, vmem_limit_bytes=48 * 2**20
        ),
        name="layer",
    )(
        queries, key_matrix_rows, value_matrix_rows, attention_output, output_gradient,
        log_sum_norm, features, adapter_down_weight, adapter_up_weight,
        attended_key_blocks, used_block_count,
    )


def solution(mesh):
    placed = (
        P("ctx", "head"),
        P("ctx", "head"),
        P("ctx", "head"),
        P("ctx", "head"),
        P("ctx", "head"),
        P("head", "ctx"),
        P("ctx", "head"),
        P(None, "head", None),
        P(None, None, "head"),
        P("ctx", None),
        P("ctx"),
    )
    return jax.shard_map(
        on_device,
        mesh=mesh,
        in_specs=placed,
        out_specs=(
            P("ctx", "head"),
            P("ctx", "head"),
            P("ctx", "head"),
            P(None, "head", None),
            P(None, None, "head"),
        ),
        check_vma=False,
    )
```

time: 147 us -> 120 us (0.82)
  Pallas kernels: 131 us -> 105 us
    pallas_call x1, Pallas kernels: 131 us -> 105 us  [on_device(): pl.pallas_call(layer_kernel, out_shape=(rows, rows, rows, down, up), in_s...]
where the time goes in v3:
time: 120 us
  Pallas kernels  105 us (88%)
  local copies, waits for them, and re-layouts  14 us (12%)
    pallas_call x1, Pallas kernels, on_device(): pl.pallas_call(layer_kernel, out_shape=(rows, rows, rows, down, up), in_s...  105 us
    unnamed x27, local copies, waits for them, and re-layouts  14 us

profile of v3, /device:TPU:1, one launch (start us, length us, event | category | flops | bytes accessed | tf_op | source)
XLA Modules:
  0.0 119.9 jit_solution(12702883259350768685)
XLA Ops:
  0.6 0.0 copy-start
  0.6 1.0 copy-done
  1.7 0.0 copy-start.1
  1.7 1.0 copy-done.1
  2.7 0.0 copy-start.2
  2.7 1.0 copy-done.2
  3.7 0.0 copy-start.3
  3.7 1.0 copy-done.3
  4.6 0.0 copy-start.4
  4.6 1.0 copy-done.4
  5.6 0.0 copy-start.5
  5.6 1.0 copy-done.5
  6.6 0.0 copy-start.6
  6.6 1.0 copy-done.6
  7.6 0.0 copy-start.7
  7.6 1.0 copy-done.7
  8.5 0.0 copy-start.8
  8.5 0.7 copy-done.8
  9.2 0.0 copy-start.9
  9.2 0.7 copy-done.9
  9.9 0.0 copy-start.10
  9.9 0.7 copy-done.10
  10.6 105.3 %layer.1 = (bf16[256,640]{1,0:T(8,128)(2,1)S(1)}, bf16[256,640]{1,0:T(8,128)(2,1)S(1)}, bf16[256,640]{1,0:T(8,128)(2,1)S(1)}, f32[3,640,128]{2,1,0:T(8,128)S(1)}, f32[3,128,640]{2,1,0:T(8,128)S(1)}) custom-call(bf16[256,640]{1,0:T(8,128)(2,1)S(1)} %copy-done.2, bf16[256,640]{1,0:T(8,128)(2,1)S(1)} %copy-done.3, bf16[256,640]{1,0:T(8,128)(2,1)S(1)} %copy-done.4, ...), custom_call_target="tpu_custom_call" | custom-call | tf_op jit(solution)/shard_map/layer/pallas_call | solution.py:531
  115.9 0.7 copy.21
  116.6 0.7 copy.22
  117.3 0.7 copy.23
  118.1 0.9 copy.24
  119.0 0.9 copy.25
Async XLA Ops:
  0.6 1.0 copy-start
  1.7 1.0 copy-start.1
  2.7 1.0 copy-start.2
  3.7 1.0 copy-start.3
  4.6 1.0 copy-start.4
  5.6 1.0 copy-start.5
  6.6 1.0 copy-start.6
  7.6 1.0 copy-start.7
  8.5 0.7 copy-start.8
  9.2 0.7 copy-start.9
  9.9 0.7 copy-start.10

commit v4 on v3

--- a/solution.py
+++ b/solution.py
@@ -20,7 +20,7 @@
 GROUPS = 8
 SHARE = TOKENS // GROUPS
 CHIPS = RING // 2
-BLOCKS = 3 * HEADS
+PIECE = HEADS * WIDTH // CHIPS
 SCALE = WIDTH ** -0.5
 LOG2E = math.log2(math.e)
 DEAD = 1e30
@@ -45,14 +45,13 @@
 
 def layer_kernel(
     q_ref, k_ref, v_ref, o_ref, g_ref, lse_ref, f_ref, down_ref, up_ref, att_ref, used_ref,
-    qg_ref, kg_ref, vg_ref, down_out, up_out,
+    qg_ref, kg_ref, vg_ref, totals,
     o_here, g_here, lse_here, f_here, down_here, up_here, in_sems,
     stats, rs, rqg, rkv, keys_t, dk_acc, dv_acc, dq_acc, dq_land, dq_out, dkv_out, rdq, rdkv,
     s_send, qg_send, kv_send, pass_send, dq_pair_send, dq_send, dkv_send,
     s_recv, qg_recv, kv_recv, pass_recv, dq_pair_recv, dq_recv, dkv_recv,
-    row_send, row_land, row_all, row_sems,
-    partial, pair_send, pair_land, sum_send, sum_land, total_all,
-    pair_sems, sum_sems, total_sems, twin_sems,
+    f_turned, projected_turned, row_send, row_land, row_all, row_sems,
+    partial, pair_send, pair_land, sum_send, sum_land, pair_sems, sum_sems, total_sems, twin_sems,
 ):
     me = lax.axis_index("ctx")
     group = lax.axis_index("head")
@@ -175,58 +174,60 @@
     send_all(query_copies)
     send_all(key_copies)
 
-    def head_copy(kind, phase, other):
+    def head_copy(kind, phase, m, other):
         if phase == 0:
-            src, dst = row_send.at[kind, other], row_land.at[kind, group]
+            src, dst = row_send.at[kind, m, other], row_land.at[kind, m, group]
         else:
-            src, dst = row_all.at[kind, group], row_all.at[kind, group]
+            src, dst = row_all.at[kind, m, group], row_all.at[kind, m, group]
         return pltpu.make_async_remote_copy(
             src_ref=src, dst_ref=dst,
-            send_sem=row_sems.at[kind, phase, 0, other],
-            recv_sem=row_sems.at[kind, phase, 1, group],
+            send_sem=row_sems.at[kind, phase, 0, m, other],
+            recv_sem=row_sems.at[kind, phase, 1, m, group],
             device_id=(me, other), device_id_type=MESH,
         )
 
-    def to_heads(kind, phase):
+    def to_heads(kind, phase, m):
         def one(step, carry):
-            head_copy(kind, phase, lax.rem(group + step, GROUPS)).start()
+            head_copy(kind, phase, m, lax.rem(group + step, GROUPS)).start()
             return carry
 
         lax.fori_loop(1, GROUPS, one, 0)
 
-    def from_heads(kind, phase):
+    def from_heads(kind, phase, m):
         def one(step, carry):
             other = lax.rem(group + step, GROUPS)
-            dst = (row_land if phase == 0 else row_all).at[kind, other]
-            landed(dst, row_sems.at[kind, phase, 1, other])
+            dst = (row_land if phase == 0 else row_all).at[kind, m, other]
+            landed(dst, row_sems.at[kind, phase, 1, m, other])
             return carry
 
         lax.fori_loop(1, GROUPS, one, 0)
 
-    def drain_heads(kind, phase):
+    def drain_heads(kind, phase, m):
         def one(step, carry):
-            head_copy(kind, phase, lax.rem(group + step, GROUPS)).wait_send()
+            head_copy(kind, phase, m, lax.rem(group + step, GROUPS)).wait_send()
             return carry
 
         lax.fori_loop(1, GROUPS, one, 0)
 
     def split_rows(kind, m, rows):
-        row_send[kind, :, m] = rows.astype(BF16).reshape(GROUPS, SHARE, WIDTH)
-
-    def sum_rows(kind):
-        row_land[kind, group] = row_send[kind, group]
-        from_heads(kind, 0)
-        row_all[kind, group] = jnp.sum(row_land[kind].astype(F32), axis=0).astype(BF16)
-        to_heads(kind, 1)
+        row_send[kind, m] = rows.astype(BF16).reshape(GROUPS, SHARE, WIDTH)
+        to_heads(kind, 0, m)
+
+    def sum_rows(kind, m):
+        row_land[kind, m, group] = row_send[kind, m, group]
+        from_heads(kind, 0, m)
+        row_all[kind, m, group] = jnp.sum(row_land[kind, m].astype(F32), axis=0).astype(BF16)
+        to_heads(kind, 1, m)
 
     def all_rows(kind, m):
-        return row_all[kind, :, m].reshape(TOKENS, WIDTH)
+        from_heads(kind, 1, m)
+        return row_all[kind, m].reshape(TOKENS, WIDTH)
 
     inputs[3].wait()
     inputs[4].wait()
     for m in range(3):
         split_rows(0, m, nn(f_here[...], down_here[m]))
-    to_heads(0, 0)
+    f_turned[...] = f_here[...].astype(F32).T.astype(BF16)
 
     my_head = lax.rem(5 * chip, CHIPS)
     working = my_head < HEADS
@@ -328,7 +329,8 @@
         use(CHIPS - 1, 0)
         close_keys(chip)
 
-    sum_rows(0)
+    for m in range(3):
+        sum_rows(0, m)
 
     @pl.when(working)
     def _other_keys():
@@ -340,7 +342,7 @@
                 compute(key_chip, chip_at(step), False)
                 return inner
 
-            lax.fori_loop(0, CHIPS, one, 0)
+            lax.fori_loop(0, CHIPS, one, 0, unroll=CHIPS)
             close_keys(key_chip)
             return carry
 
@@ -376,119 +378,128 @@
         landed(rdkv.at[h], dkv_recv.at[h])
         kg_ref[:, columns] = rdkv[h, 0]
         vg_ref[:, columns] = rdkv[h, 1]
-    from_heads(0, 1)
+    for m in range(3):
+        projected_turned[m] = all_rows(0, m).astype(F32).T.astype(BF16)
     inputs[5].wait()
 
     grads_out = (qg_ref, kg_ref, vg_ref)
+    order = (1, 2, 0)
+
+    def pair_copy(m):
+        return move(pair_send.at[m], pair_land.at[m], pair_sems.at[0, m], pair_sems.at[1, m], twin)
+
+    def sum_copy(m, other):
+        return move(
+            sum_send.at[m, other], sum_land.at[m, chip],
+            sum_sems.at[0, m, other], sum_sems.at[1, m, chip], 2 * other + core,
+        )
+
+    def total_copy(m, other):
+        return move(
+            totals.at[core, m, chip], totals.at[core, m, chip],
+            total_sems.at[0, m, other], total_sems.at[1, m, chip], 2 * other + core,
+        )
+
+    def twin_copy(m):
+        return move(
+            totals.at[core, m], totals.at[core, m], twin_sems.at[0, m], twin_sems.at[1, m], twin
+        )
+
+    def to_chips(copy, m):
+        def one(step, carry):
+            copy(m, chip_at(step)).start()
+            return carry
+
+        lax.fori_loop(1, CHIPS, one, 0)
+
+    def from_chips(land, sems, m):
+        def one(step, carry):
+            other = chip_at(step)
+            landed(land.at[m, other], sems.at[1, m, other])
+            return carry
+
+        lax.fori_loop(1, CHIPS, one, 0)
 
     def gather_rows(m):
         split_rows(1, m, nt(grads_out[m][...], up_here[m]))
 
     def up_rows(m):
-        rows = tn(all_rows(0, m), grads_out[m][...]) * adapter_scale
+        rows = nn(projected_turned[m], grads_out[m][...]) * adapter_scale
         for h in range(HEADS):
-            partial[m * HEADS + h] = rows[:, h * WIDTH : (h + 1) * WIDTH]
-
-    for m in (1, 2):
+            partial[m, h * WIDTH : (h + 1) * WIDTH] = rows[:, h * WIDTH : (h + 1) * WIDTH]
+
+        @pl.when(core == 1)
+        def _():
+            pair_send[m] = partial[m].astype(BF16)
+            pair_copy(m).start()
+
+    def down_rows(m):
+        rows = nn(f_turned[...], all_rows(1, m)) * adapter_scale
+
+        @pl.when(core == 0)
+        def _():
+            pair_send[m] = rows.astype(BF16)
+            pair_copy(m).start()
+
+        @pl.when(core == 1)
+        def _():
+            partial[m] = rows
+
+    def sum_pair(m):
+        pair_copy(m).wait_recv()
+        both = partial[m] + pair_land[m].astype(F32)
+        sum_send[m] = both.astype(BF16).reshape(CHIPS, PIECE, WIDTH)
+        to_chips(sum_copy, m)
+        sum_land[m, chip] = sum_send[m, chip]
+
+    for m in order[:2]:
         gather_rows(m)
+    for m in order[:2]:
         up_rows(m)
     for h in range(HEADS):
         landed(rdq.at[h], dq_recv.at[h])
         qg_ref[:, h * WIDTH : (h + 1) * WIDTH] = rdq[h]
     gather_rows(0)
-    to_heads(1, 0)
     up_rows(0)
-
-    twin_copy = pltpu.make_async_remote_copy(
-        src_ref=pair_send, dst_ref=pair_land, send_sem=pair_sems.at[0], recv_sem=pair_sems.at[1],
-        device_id=(twin, group), device_id_type=MESH,
-    )
-
-    def sum_copy(other):
-        return pltpu.make_async_remote_copy(
-            src_ref=sum_send.at[other], dst_ref=sum_land.at[chip],
-            send_sem=sum_sems.at[0, other], recv_sem=sum_sems.at[1, chip],
-            device_id=(2 * other + core, group), device_id_type=MESH,
-        )
-
-    def total_copy(other):
-        return pltpu.make_async_remote_copy(
-            src_ref=total_all.at[core, chip], dst_ref=total_all.at[core, chip],
-            send_sem=total_sems.at[0, other], recv_sem=total_sems.at[1, chip],
-            device_id=(2 * other + core, group), device_id_type=MESH,
-        )
-
-    def pass_copy(origin):
-        return pltpu.make_async_remote_copy(
-            src_ref=total_all.at[core, origin], dst_ref=total_all.at[core, origin],
-            send_sem=twin_sems.at[0, origin], recv_sem=twin_sems.at[1, origin],
-            device_id=(twin, group), device_id_type=MESH,
-        )
-
-    def hand_over():
-        for block in range(BLOCKS):
-            pair_send[block] = partial[block].astype(BF16)
-        twin_copy.start()
-
-    def take_over():
-        twin_copy.wait_recv()
-        for block in range(BLOCKS):
-            both = partial[block] + pair_land[block].astype(F32)
-            sum_send[block // 2, block % 2] = both.astype(BF16)
-        sum_send[CHIPS - 1, 1] = jnp.zeros((WIDTH, WIDTH), BF16)
-        for step in range(1, CHIPS):
-            sum_copy(chip_at(step)).start()
-        sum_land[chip] = sum_send[chip]
-
-    pl.when(core == 1)(hand_over)
-    sum_rows(1)
-    pl.when(core == 0)(take_over)
-    from_heads(1, 1)
+    for m in order:
+        sum_rows(1, m)
 
     @pl.when(core == 0)
-    def _down_over():
-        for m in range(3):
-            rows = tn(f_here[...], all_rows(1, m)) * adapter_scale
-            for h in range(HEADS):
-                pair_send[m * HEADS + h] = rows[h * WIDTH : (h + 1) * WIDTH].astype(BF16)
-        twin_copy.start()
+    def _up_sums():
+        for m in order:
+            sum_pair(m)
+
+    for m in order:
+        down_rows(m)
 
     @pl.when(core == 1)
-    def _down_sum():
-        for m in range(3):
-            rows = tn(f_here[...], all_rows(1, m)) * adapter_scale
-            for h in range(HEADS):
-                partial[m * HEADS + h] = rows[h * WIDTH : (h + 1) * WIDTH]
-        take_over()
-
-    for step in range(1, CHIPS):
-        other = chip_at(step)
-        landed(sum_land.at[other], sum_sems.at[1, other])
-    total_all[core, chip] = jnp.sum(sum_land[...].astype(F32), axis=0).astype(BF16)
-    for step in range(1, CHIPS):
-        total_copy(chip_at(step)).start()
-    pass_copy(chip).start()
-    for step in range(1, CHIPS):
-        other = chip_at(step)
-        landed(total_all.at[core, other], total_sems.at[1, other])
-        pass_copy(other).start()
-    for origin in range(CHIPS):
-        landed(total_all.at[1 - core, origin], twin_sems.at[1, origin])
-    for block in range(BLOCKS):
-        m, h = block // HEADS, block % HEADS
-        columns = slice(h * WIDTH, (h + 1) * WIDTH)
-        up_out[m, :, columns] = total_all[0, block // 2, block % 2].astype(F32)
-        down_out[m, columns, :] = total_all[1, block // 2, block % 2].astype(F32)
-
-    for kind in range(2):
-        for phase in range(2):
-            drain_heads(kind, phase)
-    twin_copy.wait_send()
-    for step in range(1, CHIPS):
-        sum_copy(chip_at(step)).wait_send()
-        total_copy(chip_at(step)).wait_send()
-    for origin in range(CHIPS):
-        pass_copy(origin).wait_send()
+    def _down_sums():
+        for m in order:
+            sum_pair(m)
+
+    for m in order:
+        from_chips(sum_land, sum_sems, m)
+        totals[core, m, chip] = jnp.sum(sum_land[m].astype(F32), axis=0).astype(BF16)
+        to_chips(total_copy, m)
+    for m in order:
+        from_chips(totals.at[core], total_sems, m)
+        twin_copy(m).start()
+    for m in order:
+        landed(totals.at[1 - core, m], twin_sems.at[1, m])
+
+    for m in range(3):
+        for kind in range(2):
+            for phase in range(2):
+                drain_heads(kind, phase, m)
+        pair_copy(m).wait_send()
+        twin_copy(m).wait_send()
+
+        def drain_chips(step, carry):
+            sum_copy(m, chip_at(step)).wait_send()
+            total_copy(m, chip_at(step)).wait_send()
+            return carry
+
+        lax.fori_loop(1, CHIPS, drain_chips, 0)
 
     def drain_sends(h, carry):
         for copy in query_copies(h) + key_copies(h):
@@ -507,6 +518,34 @@
             return carry
 
         lax.fori_loop(0, CHIPS, one, 0)
+
+
+def finish_kernel(q_in, k_in, v_in, totals, q_out, k_out, v_out, down_out, up_out):
+    q_out[...] = q_in[...]
+    k_out[...] = k_in[...]
+    v_out[...] = v_in[...]
+    down_out[...] = totals[1].astype(F32)
+    for m in range(3):
+        for h in range(HEADS):
+            columns = slice(h * WIDTH, (h + 1) * WIDTH)
+            up_out[m, :, columns] = totals[0, m, columns, :].astype(F32)
+
+
+def finish(query_grad, key_grad, value_grad, totals):
+    rows = jax.ShapeDtypeStruct(query_grad.shape, BF16)
+    vmem = pl.BlockSpec(memory_space=pltpu.VMEM)
+    return pl.pallas_call(
+        finish_kernel,
+        out_shape=(
+            rows, rows, rows,
+            jax.ShapeDtypeStruct((3, HEADS * WIDTH, WIDTH), F32),
+            jax.ShapeDtypeStruct((3, WIDTH, HEADS * WIDTH), F32),
+        ),
+        in_specs=[vmem] * 4,
+        out_specs=(vmem,) * 5,
+        compiler_params=pltpu.CompilerParams(vmem_limit_bytes=60 * 2**20),
+        name="finish",
+    )(query_grad, key_grad, value_grad, totals.reshape(2, 3, HEADS * WIDTH, WIDTH))
 
 
 def on_device(
@@ -525,14 +564,13 @@
     vmem = pl.BlockSpec(memory_space=pltpu.VMEM)
     smem = pl.BlockSpec(memory_space=pltpu.SMEM)
     rows = jax.ShapeDtypeStruct((TOKENS, HEADS * WIDTH), BF16)
-    down = jax.ShapeDtypeStruct((3, HEADS * WIDTH, WIDTH), F32)
-    up = jax.ShapeDtypeStruct((3, WIDTH, HEADS * WIDTH), F32)
+    totals = jax.ShapeDtypeStruct((2, 3, CHIPS, PIECE, WIDTH), BF16)
     dma = pltpu.SemaphoreType.DMA
-    return pl.pallas_call(
+    results = pl.pallas_call(
         layer_kernel,
-        out_shape=(rows, rows, rows, down, up),
-        in_specs=[pl.BlockSpec(memory_space=pl.ANY)] * 9 + [smem] * 2,
-        out_specs=(vmem,) * 5,
+        out_shape=(rows, rows, rows, totals),
+        in_specs=[pl.BlockSpec(memory_space=pltpu.HBM)] * 9 + [smem] * 2,
+        out_specs=(vmem,) * 4,
         scratch_shapes=[
             pltpu.VMEM((TOKENS, HEADS * WIDTH), BF16),
             pltpu.VMEM((TOKENS, HEADS * WIDTH), BF16),
@@ -558,20 +596,21 @@
             dma((CHIPS,)), dma((CHIPS,)), dma((CHIPS,)),
             dma((CHIPS,)), dma((CHIPS,)), dma((CHIPS,)), dma((2, CHIPS)),
             dma((CHIPS,)), dma((HEADS,)), dma((HEADS,)),
-            pltpu.VMEM((2, GROUPS, 3, SHARE, WIDTH), BF16),
-            pltpu.VMEM((2, GROUPS, 3, SHARE, WIDTH), BF16),
-            pltpu.VMEM((2, GROUPS, 3, SHARE, WIDTH), BF16),
-            dma((2, 2, 2, GROUPS)),
-            pltpu.VMEM((BLOCKS, WIDTH, WIDTH), F32),
-            pltpu.VMEM((BLOCKS, WIDTH, WIDTH), BF16),
-            pltpu.VMEM((BLOCKS, WIDTH, WIDTH), BF16),
-            pltpu.VMEM((CHIPS, 2, WIDTH, WIDTH), BF16),
-            pltpu.VMEM((CHIPS, 2, WIDTH, WIDTH), BF16),
-            pltpu.VMEM((2, CHIPS, 2, WIDTH, WIDTH), BF16),
-            dma((2,)), dma((2, CHIPS)), dma((2, CHIPS)), dma((2, CHIPS)),
+            pltpu.VMEM((HEADS * WIDTH, TOKENS), BF16),
+            pltpu.VMEM((3, WIDTH, TOKENS), BF16),
+            pltpu.VMEM((2, 3, GROUPS, SHARE, WIDTH), BF16),
+            pltpu.VMEM((2, 3, GROUPS, SHARE, WIDTH), BF16),
+            pltpu.VMEM((2, 3, GROUPS, SHARE, WIDTH), BF16),
+            dma((2, 2, 2, 3, GROUPS)),
+            pltpu.VMEM((3, HEADS * WIDTH, WIDTH), F32),
+            pltpu.VMEM((3, HEADS * WIDTH, WIDTH), BF16),
+            pltpu.VMEM((3, HEADS * WIDTH, WIDTH), BF16),
+            pltpu.VMEM((3, CHIPS, PIECE, WIDTH), BF16),
+            pltpu.VMEM((3, CHIPS, PIECE, WIDTH), BF16),
+            dma((2, 3)), dma((2, 3, CHIPS)), dma((2, 3, CHIPS)), dma((2, 3)),
         ],
         compiler_params=pltpu.CompilerParams(
-            collective_id=0, has_side_effects=True, vmem_limit_bytes=48 * 2**20
+            collective_id=0, has_side_effects=True, vmem_limit_bytes=60 * 2**20
         ),
         name="layer",
     )(
@@ -579,6 +618,7 @@
         log_sum_norm, features, adapter_down_weight, adapter_up_weight,
         attended_key_blocks, used_block_count,
     )
+    return finish(*results)
 
 
 def solution(mesh):

time: 120 us -> 101 us (0.84)
  local copies, waits for them, and re-layouts: 14 us -> 0 us
  Pallas kernels: 105 us -> 100 us
    unnamed x27 -> x0, local copies, waits for them, and re-layouts: 14 us -> none
    pallas_call x1 -> x2, Pallas kernels: 105 us -> 100 us  [the longest x1 97.4 us: on_device(): pl.pallas_call(layer_kernel, out_shape=(rows, rows, rows, totals), in_spe...]
where the time goes in v4:
time: 101 us
  Pallas kernels  100 us (99%)
    pallas_call x1, Pallas kernels, on_device(): pl.pallas_call(layer_kernel, out_shape=(rows, rows, rows, totals), in_spe...  97.4 us
    pallas_call x1, Pallas kernels, finish(): pl.pallas_call(finish_kernel, out_shape=(rows, rows, rows, jax.ShapeDtype...  3.13 us

profile of v4, /device:TPU:1, one launch (start us, length us, event | category | flops | bytes accessed | tf_op | source)
XLA Modules:
  0.0 101.1 jit_solution(4101129813669071506)
XLA Ops:
  0.6 97.4 %layer.1 = (bf16[256,640]{1,0:T(8,128)(2,1)}, bf16[256,640]{1,0:T(8,128)(2,1)}, bf16[256,640]{1,0:T(8,128)(2,1)}, bf16[2,3,8,80,128]{4,3,2,1,0:T(8,128)(2,1)}) custom-call(bf16[256,640]{1,0:T(8,128)(2,1)} %q_ref.1, bf16[256,640]{1,0:T(8,128)(2,1)} %k_ref.1, bf16[256,640]{1,0:T(8,128)(2,1)} %v_ref.1, bf16[256,640]{1,0:T(8,128)(2,1)} %o_ref.1, ...), custom_call_target="tpu_custom_call" | custom-call | tf_op jit(solution)/shard_map/layer/pallas_call | solution.py:569
  98.0 3.1 %finish.1 = (bf16[256,640]{1,0:T(8,128)(2,1)}, bf16[256,640]{1,0:T(8,128)(2,1)}, bf16[256,640]{1,0:T(8,128)(2,1)}, f32[3,640,128]{2,1,0:T(8,128)}, f32[3,128,640]{2,1,0:T(8,128)}) custom-call(bf16[256,640]{1,0:T(8,128)(2,1)} %get-tuple-element.9.q_in, bf16[256,640]{1,0:T(8,128)(2,1)} %get-tuple-element.10.k_in, bf16[256,640]{1,0:T(8,128)(2,1)} %get-tuple-element.11.v_in, ...), custom_call_target="tpu_custom_call" | custom-call | tf_op jit(solution)/shard_map/finish/pallas_call | solution.py:537

commit v5 on v4

--- a/solution.py
+++ b/solution.py
@@ -17,6 +17,8 @@
 TOKENS = 256
 RING = 16
 BLOCK = 128
+EARLY = 4
+LATE = 1
 GROUPS = 8
 SHARE = TOKENS // GROUPS
 CHIPS = RING // 2
@@ -50,7 +52,7 @@
     stats, rs, rqg, rkv, keys_t, dk_acc, dv_acc, dq_acc, dq_land, dq_out, dkv_out, rdq, rdkv,
     s_send, qg_send, kv_send, pass_send, dq_pair_send, dq_send, dkv_send,
     s_recv, qg_recv, kv_recv, pass_recv, dq_pair_recv, dq_recv, dkv_recv,
-    f_turned, projected_turned, row_send, row_land, row_all, row_sems,
+    f_turned, f_twin, projected_turned, row_twin, row_twin_sems, f_twin_sems, row_send, row_land, row_all, row_sems,
     partial, pair_send, pair_land, sum_send, sum_land, pair_sems, sum_sems, total_sems, twin_sems,
 ):
     me = lax.axis_index("ctx")
@@ -114,6 +116,44 @@
     ]
     for copy in inputs:
         copy.start()
+
+    pl.semaphore_wait(barrier, CHIPS + GROUPS - 1)
+
+    def query_copies(h):
+        target = 2 * lax.rem(5 * h, CHIPS) + core
+        lanes = lane_slice(h)
+        return (
+            (q_ref.at[:, lanes], rqg.at[chip, core, 0], qg_send.at[0, h], qg_recv.at[chip], target),
+            (g_ref.at[:, lanes], rqg.at[chip, core, 1], qg_send.at[1, h], qg_recv.at[chip], target),
+        )
+
+    def stats_copies(h):
+        target = 2 * lax.rem(5 * h, CHIPS) + core
+        return ((stats.at[h], rs.at[chip, core], s_send.at[h], s_recv.at[chip], target),)
+
+    def key_copies(h):
+        target = 2 * lax.rem(5 * h, CHIPS) + core
+        lanes = lane_slice(h)
+        return (
+            (k_ref.at[:, lanes], rkv.at[chip, 0], kv_send.at[0, h], kv_recv.at[chip], target),
+            (v_ref.at[:, lanes], rkv.at[chip, 1], kv_send.at[1, h], kv_recv.at[chip], target),
+        )
+
+    def send_some(copies, begin, end):
+        def one(step, carry):
+            h = lax.rem(5 * lax.rem(chip - step + CHIPS, CHIPS), CHIPS)
+
+            @pl.when(h < HEADS)
+            def _():
+                for copy in copies(h):
+                    start(*copy)
+
+            return carry
+
+        lax.fori_loop(begin, end, one, 0)
+
+    send_some(key_copies, 0, EARLY)
+    send_some(query_copies, 0, CHIPS)
 
     lane = lax.broadcasted_iota(jnp.int32, (1, TOKENS), 1)
     words = [[jnp.int32(0), jnp.int32(0)], [jnp.int32(0), jnp.int32(0)]]
@@ -139,40 +179,8 @@
             [norm, row_dot, codes[0], codes[1], jnp.zeros((4, TOKENS), F32)], axis=0
         )
 
-    pl.semaphore_wait(barrier, CHIPS + GROUPS - 1)
-
-    def query_copies(h):
-        target = 2 * lax.rem(5 * h, CHIPS) + core
-        lanes = lane_slice(h)
-        return (
-            (stats.at[h], rs.at[chip, core], s_send.at[h], s_recv.at[chip], target),
-            (q_ref.at[:, lanes], rqg.at[chip, core, 0], qg_send.at[0, h], qg_recv.at[chip], target),
-            (g_ref.at[:, lanes], rqg.at[chip, core, 1], qg_send.at[1, h], qg_recv.at[chip], target),
-        )
-
-    def key_copies(h):
-        target = 2 * lax.rem(5 * h, CHIPS) + core
-        lanes = lane_slice(h)
-        return (
-            (k_ref.at[:, lanes], rkv.at[chip, 0], kv_send.at[0, h], kv_recv.at[chip], target),
-            (v_ref.at[:, lanes], rkv.at[chip, 1], kv_send.at[1, h], kv_recv.at[chip], target),
-        )
-
-    def send_all(copies):
-        def one(step, carry):
-            h = lax.rem(5 * lax.rem(chip - step + CHIPS, CHIPS), CHIPS)
-
-            @pl.when(h < HEADS)
-            def _():
-                for copy in copies(h):
-                    start(*copy)
-
-            return carry
-
-        lax.fori_loop(0, CHIPS, one, 0)
-
-    send_all(query_copies)
-    send_all(key_copies)
+    send_some(stats_copies, 0, CHIPS)
+    send_some(key_copies, EARLY, CHIPS)
 
     def head_copy(kind, phase, m, other):
         if phase == 0:
@@ -228,6 +236,11 @@
     for m in range(3):
         split_rows(0, m, nn(f_here[...], down_here[m]))
     f_turned[...] = f_here[...].astype(F32).T.astype(BF16)
+    f_copy = move(f_turned, f_twin, f_twin_sems.at[0], f_twin_sems.at[1], twin)
+
+    @pl.when(core == 0)
+    def _():
+        f_copy.start()
 
     my_head = lax.rem(5 * chip, CHIPS)
     working = my_head < HEADS
@@ -252,7 +265,7 @@
         return (dkv_out.at[origin], rdkv.at[my_head],
                 dkv_send.at[origin], dkv_recv.at[my_head], 2 * origin + core)
 
-    def compute(key_chip, origin, first):
+    def compute(key_chip, slot, origin, first):
         keys = rkv[key_chip, 0]
         queries = rqg[origin, :, 0].reshape(2 * TOKENS, WIDTH)
         grads = rqg[origin, :, 1].reshape(2 * TOKENS, WIDTH)
@@ -279,9 +292,9 @@
             )
         low = jnp.concatenate(low_parts, axis=0)
         score_grad = jnp.concatenate(grad_parts, axis=0)
-        dv_acc[...] += nn(low, grads)
-        dk_acc[...] += nn(score_grad, queries)
-        dq_part = nn(keys_t[...], score_grad)
+        dv_acc[slot] += nn(low, grads)
+        dk_acc[slot] += nn(score_grad, queries)
+        dq_part = nn(keys_t[slot], score_grad)
         for side in range(2):
             piece = dq_part[:, side * TOKENS : (side + 1) * TOKENS]
             if first:
@@ -289,45 +302,46 @@
             else:
                 dq_acc[origin, side] += piece
 
-    def open_keys(key_chip):
+    def open_keys(key_chip, slot):
         landed(rkv.at[key_chip], kv_recv.at[key_chip])
-        keys_t[...] = rkv[key_chip, 0].astype(F32).T.astype(BF16)
-        dk_acc[...] = jnp.zeros_like(dk_acc)
-        dv_acc[...] = jnp.zeros_like(dv_acc)
-
-    def close_keys(key_chip):
-        dkv_out[key_chip, 0] = dk_acc[...].astype(BF16)
-        dkv_out[key_chip, 1] = dv_acc[...].astype(BF16)
+        keys_t[slot] = rkv[key_chip, 0].astype(F32).T.astype(BF16)
+        dk_acc[slot] = jnp.zeros((TOKENS, WIDTH), F32)
+        dv_acc[slot] = jnp.zeros((TOKENS, WIDTH), F32)
+
+    def close_keys(key_chip, slot):
+        dkv_out[key_chip, 0] = dk_acc[slot].astype(BF16)
+        dkv_out[key_chip, 1] = dv_acc[slot].astype(BF16)
         start(*dkv_copy(key_chip))
 
     @pl.when(working)
     def _first_keys():
-        open_keys(chip)
-
-        def receive(step, carry):
+        def receive(step):
             origin = chip_at(step)
             landed(rs.at[origin, core], s_recv.at[origin])
             landed(rqg.at[origin, core], qg_recv.at[origin])
             for copy in pass_copies(origin):
                 move(*copy).start()
-            return carry
-
-        def use(step, carry):
+
+        def use(step):
             origin = chip_at(step)
             landed(rs.at[origin, 1 - core], pass_recv.at[0, origin])
             landed(rqg.at[origin, 1 - core], pass_recv.at[1, origin])
-            compute(chip, origin, True)
-            return carry
-
-        receive(0, 0)
+            for slot in range(EARLY):
+                compute(chip_at(slot), slot, origin, slot == 0)
+
+        for slot in range(EARLY):
+            open_keys(chip_at(slot), slot)
+        receive(0)
 
         def both(step, carry):
-            receive(step, carry)
-            return use(step - 1, carry)
+            receive(step)
+            use(step - 1)
+            return carry
 
         lax.fori_loop(1, CHIPS, both, 0)
-        use(CHIPS - 1, 0)
-        close_keys(chip)
+        use(CHIPS - 1)
+        for slot in range(EARLY):
+            close_keys(chip_at(slot), slot)
 
     for m in range(3):
         sum_rows(0, m)
@@ -336,51 +350,51 @@
     def _other_keys():
         def middle(turn, carry):
             key_chip = chip_at(turn)
-            open_keys(key_chip)
+            open_keys(key_chip, 0)
 
             def one(step, inner):
-                compute(key_chip, chip_at(step), False)
+                compute(key_chip, 0, chip_at(step), False)
                 return inner
 
             lax.fori_loop(0, CHIPS, one, 0, unroll=CHIPS)
-            close_keys(key_chip)
-            return carry
-
-        lax.fori_loop(1, CHIPS - 1, middle, 0)
-
-        key_chip = chip_at(CHIPS - 1)
-        open_keys(key_chip)
-
-        def finish(step):
+            close_keys(key_chip, 0)
+            return carry
+
+        lax.fori_loop(EARLY, CHIPS - LATE, middle, 0)
+
+        late = [chip_at(CHIPS - LATE + slot) for slot in range(LATE)]
+        for slot in range(LATE):
+            open_keys(late[slot], slot)
+
+        def finish_query(step):
             origin = chip_at(step)
             landed(dq_land.at[origin], dq_pair_recv.at[origin])
             total = dq_acc[origin, core] + dq_land[origin]
             dq_out[origin] = total.T.astype(BF16)
             start(*dq_copy(origin))
 
-        def last(step, carry):
-            origin = chip_at(step)
-            compute(key_chip, origin, False)
-            move(*dq_pair_copy(origin)).start()
-
-            @pl.when(step > 0)
-            def _():
-                finish(step - 1)
-
-            return carry
-
-        lax.fori_loop(0, CHIPS, last, 0)
-        close_keys(key_chip)
-        finish(CHIPS - 1)
+        for step in range(0, CHIPS, 2):
+            for place in (step, step + 1):
+                for slot in range(LATE):
+                    compute(late[slot], slot, chip_at(place), False)
+            for place in (step, step + 1):
+                move(*dq_pair_copy(chip_at(place))).start()
+            if step > 0:
+                finish_query(step - 2)
+                finish_query(step - 1)
+        for slot in range(LATE):
+            close_keys(late[slot], slot)
+        finish_query(CHIPS - 2)
+        finish_query(CHIPS - 1)
 
     for h in range(HEADS):
         columns = slice(h * WIDTH, (h + 1) * WIDTH)
         landed(rdkv.at[h], dkv_recv.at[h])
         kg_ref[:, columns] = rdkv[h, 0]
         vg_ref[:, columns] = rdkv[h, 1]
+    inputs[5].wait()
     for m in range(3):
         projected_turned[m] = all_rows(0, m).astype(F32).T.astype(BF16)
-    inputs[5].wait()
 
     grads_out = (qg_ref, kg_ref, vg_ref)
     order = (1, 2, 0)
@@ -433,49 +447,50 @@
             pair_send[m] = partial[m].astype(BF16)
             pair_copy(m).start()
 
-    def down_rows(m):
-        rows = nn(f_turned[...], all_rows(1, m)) * adapter_scale
-
-        @pl.when(core == 0)
-        def _():
-            pair_send[m] = rows.astype(BF16)
-            pair_copy(m).start()
-
-        @pl.when(core == 1)
-        def _():
-            partial[m] = rows
-
-    def sum_pair(m):
-        pair_copy(m).wait_recv()
-        both = partial[m] + pair_land[m].astype(F32)
-        sum_send[m] = both.astype(BF16).reshape(CHIPS, PIECE, WIDTH)
+    def row_copy(m):
+        return move(
+            row_all.at[1, m], row_twin.at[m], row_twin_sems.at[0, m], row_twin_sems.at[1, m], twin
+        )
+
+    def to_sums(m, rows):
+        sum_send[m] = rows.astype(BF16).reshape(CHIPS, PIECE, WIDTH)
         to_chips(sum_copy, m)
         sum_land[m, chip] = sum_send[m, chip]
 
+    def up_sum(m):
+        pair_copy(m).wait_recv()
+        to_sums(m, partial[m] + pair_land[m].astype(F32))
+
+    def down_sum(m):
+        rows = nn(f_turned[...], all_rows(1, m))
+        row_copy(m).wait_recv()
+        rows += nn(f_twin[...], row_twin[m].reshape(TOKENS, WIDTH))
+        to_sums(m, rows * adapter_scale)
+
     for m in order[:2]:
         gather_rows(m)
-    for m in order[:2]:
-        up_rows(m)
     for h in range(HEADS):
         landed(rdq.at[h], dq_recv.at[h])
         qg_ref[:, h * WIDTH : (h + 1) * WIDTH] = rdq[h]
     gather_rows(0)
-    up_rows(0)
+    for m in order:
+        up_rows(m)
     for m in order:
         sum_rows(1, m)
 
     @pl.when(core == 0)
     def _up_sums():
         for m in order:
-            sum_pair(m)
-
-    for m in order:
-        down_rows(m)
+            up_sum(m)
+        for m in order:
+            from_heads(1, 1, m)
+            row_copy(m).start()
 
     @pl.when(core == 1)
     def _down_sums():
+        f_copy.wait_recv()
         for m in order:
-            sum_pair(m)
+            down_sum(m)
 
     for m in order:
         from_chips(sum_land, sum_sems, m)
@@ -491,7 +506,6 @@
         for kind in range(2):
             for phase in range(2):
                 drain_heads(kind, phase, m)
-        pair_copy(m).wait_send()
         twin_copy(m).wait_send()
 
         def drain_chips(step, carry):
@@ -501,8 +515,19 @@
 
         lax.fori_loop(1, CHIPS, drain_chips, 0)
 
+    @pl.when(core == 0)
+    def _drain_rows():
+        f_copy.wait_send()
+        for m in range(3):
+            row_copy(m).wait_send()
+
+    @pl.when(core == 1)
+    def _drain_pairs():
+        for m in range(3):
+            pair_copy(m).wait_send()
+
     def drain_sends(h, carry):
-        for copy in query_copies(h) + key_copies(h):
+        for copy in query_copies(h) + stats_copies(h) + key_copies(h):
             sent(*copy)
         return carry
 
@@ -583,9 +608,9 @@
             pltpu.VMEM((CHIPS, 2, 8, TOKENS), F32),
             pltpu.VMEM((CHIPS, 2, 2, TOKENS, WIDTH), BF16),
             pltpu.VMEM((CHIPS, 2, TOKENS, WIDTH), BF16),
-            pltpu.VMEM((WIDTH, TOKENS), BF16),
-            pltpu.VMEM((TOKENS, WIDTH), F32),
-            pltpu.VMEM((TOKENS, WIDTH), F32),
+            pltpu.VMEM((EARLY, WIDTH, TOKENS), BF16),
+            pltpu.VMEM((EARLY, TOKENS, WIDTH), F32),
+            pltpu.VMEM((EARLY, TOKENS, WIDTH), F32),
             pltpu.VMEM((CHIPS, 2, WIDTH, TOKENS), F32),
             pltpu.VMEM((CHIPS, WIDTH, TOKENS), F32),
             pltpu.VMEM((CHIPS, TOKENS, WIDTH), BF16),
@@ -597,7 +622,10 @@
             dma((CHIPS,)), dma((CHIPS,)), dma((CHIPS,)), dma((2, CHIPS)),
             dma((CHIPS,)), dma((HEADS,)), dma((HEADS,)),
             pltpu.VMEM((HEADS * WIDTH, TOKENS), BF16),
+            pltpu.VMEM((HEADS * WIDTH, TOKENS), BF16),
             pltpu.VMEM((3, WIDTH, TOKENS), BF16),
+            pltpu.VMEM((3, GROUPS, SHARE, WIDTH), BF16),
+            dma((2, 3)), dma((2,)),
             pltpu.VMEM((2, 3, GROUPS, SHARE, WIDTH), BF16),
             pltpu.VMEM((2, 3, GROUPS, SHARE, WIDTH), BF16),
             pltpu.VMEM((2, 3, GROUPS, SHARE, WIDTH), BF16),

time: 101 us -> 97.8 us (0.968)
  Pallas kernels: 100 us -> 97 us
    pallas_call x1, Pallas kernels: 97.4 us -> 93.9 us  [on_device(): pl.pallas_call(layer_kernel, out_shape=(rows, rows, rows, totals), in_spe...]
where the time goes in v5:
time: 97.8 us; the launch traced here: 97.6 us
  Pallas kernels  97 us (99%)
    pallas_call x1, Pallas kernels, on_device(): pl.pallas_call(layer_kernel, out_shape=(rows, rows, rows, totals), in_spe...  93.9 us
    pallas_call x1, Pallas kernels, finish(): pl.pallas_call(finish_kernel, out_shape=(rows, rows, rows, jax.ShapeDtype...  3.13 us

profile of v5, /device:TPU:1, one launch (start us, length us, event | category | flops | bytes accessed | tf_op | source)
XLA Modules:
  0.0 97.6 jit_solution(16759416732063122776)
XLA Ops:
  0.6 93.9 %layer.1 = (bf16[256,640]{1,0:T(8,128)(2,1)}, bf16[256,640]{1,0:T(8,128)(2,1)}, bf16[256,640]{1,0:T(8,128)(2,1)}, bf16[2,3,8,80,128]{4,3,2,1,0:T(8,128)(2,1)}) custom-call(bf16[256,640]{1,0:T(8,128)(2,1)} %q_ref.1, bf16[256,640]{1,0:T(8,128)(2,1)} %k_ref.1, bf16[256,640]{1,0:T(8,128)(2,1)} %v_ref.1, bf16[256,640]{1,0:T(8,128)(2,1)} %o_ref.1, ...), custom_call_target="tpu_custom_call" | custom-call | tf_op jit(solution)/shard_map/layer/pallas_call | solution.py:594
  94.5 3.1 %finish.1 = (bf16[256,640]{1,0:T(8,128)(2,1)}, bf16[256,640]{1,0:T(8,128)(2,1)}, bf16[256,640]{1,0:T(8,128)(2,1)}, f32[3,640,128]{2,1,0:T(8,128)}, f32[3,128,640]{2,1,0:T(8,128)}) custom-call(bf16[256,640]{1,0:T(8,128)(2,1)} %get-tuple-element.9.q_in, bf16[256,640]{1,0:T(8,128)(2,1)} %get-tuple-element.10.k_in, bf16[256,640]{1,0:T(8,128)(2,1)} %get-tuple-element.11.v_in, ...), custom_call_target="tpu_custom_call" | custom-call | tf_op jit(solution)/shard_map/finish/pallas_call | solution.py:562

commit v6 on v5

--- a/solution.py
+++ b/solution.py
@@ -47,7 +47,8 @@
 
 def layer_kernel(
     q_ref, k_ref, v_ref, o_ref, g_ref, lse_ref, f_ref, down_ref, up_ref, att_ref, used_ref,
-    qg_ref, kg_ref, vg_ref, totals,
+    q_out, k_out, v_out, totals,
+    qg_ref, kg_ref, vg_ref, out_sems,
     o_here, g_here, lse_here, f_here, down_here, up_here, in_sems,
     stats, rs, rqg, rkv, keys_t, dk_acc, dv_acc, dq_acc, dq_land, dq_out, dkv_out, rdq, rdkv,
     s_send, qg_send, kv_send, pass_send, dq_pair_send, dq_send, dkv_send,
@@ -176,7 +177,7 @@
         row_dot = jnp.sum(product.T, axis=0, keepdims=True)
         norm = lse_here[h : h + 1, :] * LOG2E
         stats[h] = jnp.concatenate(
-            [norm, row_dot, codes[0], codes[1], jnp.zeros((4, TOKENS), F32)], axis=0
+            [norm, row_dot, codes[0], codes[1]], axis=0
         )
 
     send_some(stats_copies, 0, CHIPS)
@@ -334,17 +335,26 @@
         receive(0)
 
         def both(step, carry):
-            receive(step)
+            @pl.when(step < CHIPS)
+            def _():
+                receive(step)
+
+            @pl.when(step == 5)
+            def _():
+                for m in range(3):
+                    sum_rows(0, m)
+
             use(step - 1)
             return carry
 
-        lax.fori_loop(1, CHIPS, both, 0)
-        use(CHIPS - 1)
+        lax.fori_loop(1, CHIPS + 1, both, 0)
         for slot in range(EARLY):
             close_keys(chip_at(slot), slot)
 
-    for m in range(3):
-        sum_rows(0, m)
+    @pl.when(my_head >= HEADS)
+    def _idle():
+        for m in range(3):
+            sum_rows(0, m)
 
     @pl.when(working)
     def _other_keys():
@@ -373,15 +383,21 @@
             dq_out[origin] = total.T.astype(BF16)
             start(*dq_copy(origin))
 
-        for step in range(0, CHIPS, 2):
-            for place in (step, step + 1):
+        def last(pair, carry):
+            for place in (2 * pair, 2 * pair + 1):
                 for slot in range(LATE):
                     compute(late[slot], slot, chip_at(place), False)
-            for place in (step, step + 1):
+            for place in (2 * pair, 2 * pair + 1):
                 move(*dq_pair_copy(chip_at(place))).start()
-            if step > 0:
-                finish_query(step - 2)
-                finish_query(step - 1)
+
+            @pl.when(pair > 0)
+            def _():
+                finish_query(2 * pair - 2)
+                finish_query(2 * pair - 1)
+
+            return carry
+
+        lax.fori_loop(0, CHIPS // 2, last, 0)
         for slot in range(LATE):
             close_keys(late[slot], slot)
         finish_query(CHIPS - 2)
@@ -392,6 +408,12 @@
         landed(rdkv.at[h], dkv_recv.at[h])
         kg_ref[:, columns] = rdkv[h, 0]
         vg_ref[:, columns] = rdkv[h, 1]
+    outputs = [
+        pltpu.make_async_copy(src, dst, out_sems.at[index])
+        for index, (src, dst) in enumerate(((qg_ref, q_out), (kg_ref, k_out), (vg_ref, v_out)))
+    ]
+    outputs[1].start()
+    outputs[2].start()
     inputs[5].wait()
     for m in range(3):
         projected_turned[m] = all_rows(0, m).astype(F32).T.astype(BF16)
@@ -472,6 +494,7 @@
     for h in range(HEADS):
         landed(rdq.at[h], dq_recv.at[h])
         qg_ref[:, h * WIDTH : (h + 1) * WIDTH] = rdq[h]
+    outputs[0].start()
     gather_rows(0)
     for m in order:
         up_rows(m)
@@ -502,6 +525,8 @@
     for m in order:
         landed(totals.at[1 - core, m], twin_sems.at[1, m])
 
+    for copy in outputs:
+        copy.wait()
     for m in range(3):
         for kind in range(2):
             for phase in range(2):
@@ -545,15 +570,28 @@
         lax.fori_loop(0, CHIPS, one, 0)
 
 
-def finish_kernel(q_in, k_in, v_in, totals, q_out, k_out, v_out, down_out, up_out):
-    q_out[...] = q_in[...]
-    k_out[...] = k_in[...]
-    v_out[...] = v_in[...]
-    down_out[...] = totals[1].astype(F32)
+def finish_kernel(
+    q_in, k_in, v_in, totals, q_out, k_out, v_out, down_out, up_out, down_here, up_here, sems
+):
+    def leave(index, src, dst):
+        copy = pltpu.make_async_copy(src, dst, sems.at[index])
+        copy.start()
+        return copy
+
+    copies = [
+        leave(index, src, dst)
+        for index, (src, dst) in enumerate(((q_in, q_out), (k_in, k_out), (v_in, v_out)))
+    ]
+    for m in range(3):
+        down_here[m] = totals[1, m].astype(F32)
+        copies.append(leave(3 + m, down_here.at[m], down_out.at[m]))
     for m in range(3):
         for h in range(HEADS):
             columns = slice(h * WIDTH, (h + 1) * WIDTH)
-            up_out[m, :, columns] = totals[0, m, columns, :].astype(F32)
+            up_here[m, :, columns] = totals[0, m, columns, :].astype(F32)
+        copies.append(leave(6 + m, up_here.at[m], up_out.at[m]))
+    for copy in copies:
+        copy.wait()
 
 
 def finish(query_grad, key_grad, value_grad, totals):
@@ -567,7 +605,12 @@
             jax.ShapeDtypeStruct((3, WIDTH, HEADS * WIDTH), F32),
         ),
         in_specs=[vmem] * 4,
-        out_specs=(vmem,) * 5,
+        out_specs=(pl.BlockSpec(memory_space=pltpu.HBM),) * 5,
+        scratch_shapes=[
+            pltpu.VMEM((3, HEADS * WIDTH, WIDTH), F32),
+            pltpu.VMEM((3, WIDTH, HEADS * WIDTH), F32),
+            pltpu.SemaphoreType.DMA((9,)),
+        ],
         compiler_params=pltpu.CompilerParams(vmem_limit_bytes=60 * 2**20),
         name="finish",
     )(query_grad, key_grad, value_grad, totals.reshape(2, 3, HEADS * WIDTH, WIDTH))
@@ -595,8 +638,12 @@
         layer_kernel,
         out_shape=(rows, rows, rows, totals),
         in_specs=[pl.BlockSpec(memory_space=pltpu.HBM)] * 9 + [smem] * 2,
-        out_specs=(vmem,) * 4,
+        out_specs=(pl.BlockSpec(memory_space=pltpu.HBM),) * 3 + (vmem,),
         scratch_shapes=[
+            pltpu.VMEM((TOKENS, HEADS * WIDTH), BF16),
+            pltpu.VMEM((TOKENS, HEADS * WIDTH), BF16),
+            pltpu.VMEM((TOKENS, HEADS * WIDTH), BF16),
+            dma((3,)),
             pltpu.VMEM((TOKENS, HEADS * WIDTH), BF16),
             pltpu.VMEM((TOKENS, HEADS * WIDTH), BF16),
             pltpu.VMEM((HEADS, TOKENS), F32),
@@ -604,8 +651,8 @@
             pltpu.VMEM((3, HEADS * WIDTH, WIDTH), BF16),
             pltpu.VMEM((3, WIDTH, HEADS * WIDTH), BF16),
             dma((6,)),
-            pltpu.VMEM((HEADS, 8, TOKENS), F32),
-            pltpu.VMEM((CHIPS, 2, 8, TOKENS), F32),
+            pltpu.VMEM((HEADS, 4, TOKENS), F32),
+            pltpu.VMEM((CHIPS, 2, 4, TOKENS), F32),
             pltpu.VMEM((CHIPS, 2, 2, TOKENS, WIDTH), BF16),
             pltpu.VMEM((CHIPS, 2, TOKENS, WIDTH), BF16),
             pltpu.VMEM((EARLY, WIDTH, TOKENS), BF16),

time: 97.8 us -> 96.4 us (0.986)
  Pallas kernels: 97 us -> 95.6 us
    pallas_call x1, Pallas kernels: 93.9 us -> 92.4 us  [on_device(): pl.pallas_call(layer_kernel, out_shape=(rows, rows, rows, totals), in_spe...]
where the time goes in v6:
time: 96.4 us; the launch traced here: 96.2 us
  Pallas kernels  95.6 us (99%)
    pallas_call x1, Pallas kernels, on_device(): pl.pallas_call(layer_kernel, out_shape=(rows, rows, rows, totals), in_spe...  92.4 us
    pallas_call x1, Pallas kernels, finish(): pl.pallas_call(finish_kernel, out_shape=(rows, rows, rows, jax.ShapeDtype...  3.17 us

profile of v6, /device:TPU:1, one launch (start us, length us, event | category | flops | bytes accessed | tf_op | source)
XLA Modules:
  0.0 96.2 jit_solution(6735018079150905289)
XLA Ops:
  0.6 92.4 %layer.1 = (bf16[256,640]{1,0:T(8,128)(2,1)}, bf16[256,640]{1,0:T(8,128)(2,1)}, bf16[256,640]{1,0:T(8,128)(2,1)}, bf16[2,3,8,80,128]{4,3,2,1,0:T(8,128)(2,1)}) custom-call(bf16[256,640]{1,0:T(8,128)(2,1)} %q_ref.1, bf16[256,640]{1,0:T(8,128)(2,1)} %k_ref.1, bf16[256,640]{1,0:T(8,128)(2,1)} %v_ref.1, bf16[256,640]{1,0:T(8,128)(2,1)} %o_ref.1, ...), custom_call_target="tpu_custom_call" | custom-call | tf_op jit(solution)/shard_map/layer/pallas_call | solution.py:637
  93.1 3.2 %finish.1 = (bf16[256,640]{1,0:T(8,128)(2,1)}, bf16[256,640]{1,0:T(8,128)(2,1)}, bf16[256,640]{1,0:T(8,128)(2,1)}, f32[3,640,128]{2,1,0:T(8,128)}, f32[3,128,640]{2,1,0:T(8,128)}) custom-call(bf16[256,640]{1,0:T(8,128)(2,1)} %get-tuple-element.9.q_in, bf16[256,640]{1,0:T(8,128)(2,1)} %get-tuple-element.10.k_in, bf16[256,640]{1,0:T(8,128)(2,1)} %get-tuple-element.11.v_in, ...), custom_call_target="tpu_custom_call" | custom-call | tf_op jit(solution)/shard_map/finish/pallas_call | solution.py:600

commit v7 on v6

--- a/solution.py
+++ b/solution.py
@@ -443,7 +443,7 @@
 
     def to_chips(copy, m):
         def one(step, carry):
-            copy(m, chip_at(step)).start()
+            copy(m, chip_at(CHIPS - step)).start()
             return carry
 
         lax.fori_loop(1, CHIPS, one, 0)
@@ -491,15 +491,17 @@
 
     for m in order[:2]:
         gather_rows(m)
+    for m in order[:2]:
+        up_rows(m)
     for h in range(HEADS):
         landed(rdq.at[h], dq_recv.at[h])
         qg_ref[:, h * WIDTH : (h + 1) * WIDTH] = rdq[h]
     outputs[0].start()
     gather_rows(0)
-    for m in order:
-        up_rows(m)
-    for m in order:
+    for m in order[:2]:
         sum_rows(1, m)
+    up_rows(0)
+    sum_rows(1, 0)
 
     @pl.when(core == 0)
     def _up_sums():

time: 96.4 us -> 97.1 us (level)
  no operation moved by 1% of the time
where the time goes in v7:
time: 97.1 us; the launch traced here: 96.9 us
  Pallas kernels  96.3 us (99%)
    pallas_call x1, Pallas kernels, on_device(): pl.pallas_call(layer_kernel, out_shape=(rows, rows, rows, totals), in_spe...  93.1 us
    pallas_call x1, Pallas kernels, finish(): pl.pallas_call(finish_kernel, out_shape=(rows, rows, rows, jax.ShapeDtype...  3.17 us

profile of v7, /device:TPU:1, one launch (start us, length us, event | category | flops | bytes accessed | tf_op | source)
XLA Modules:
  0.0 96.9 jit_solution(3753237640890460768)
XLA Ops:
  0.6 93.1 %layer.1 = (bf16[256,640]{1,0:T(8,128)(2,1)}, bf16[256,640]{1,0:T(8,128)(2,1)}, bf16[256,640]{1,0:T(8,128)(2,1)}, bf16[2,3,8,80,128]{4,3,2,1,0:T(8,128)(2,1)}) custom-call(bf16[256,640]{1,0:T(8,128)(2,1)} %q_ref.1, bf16[256,640]{1,0:T(8,128)(2,1)} %k_ref.1, bf16[256,640]{1,0:T(8,128)(2,1)} %v_ref.1, bf16[256,640]{1,0:T(8,128)(2,1)} %o_ref.1, ...), custom_call_target="tpu_custom_call" | custom-call | tf_op jit(solution)/shard_map/layer/pallas_call | solution.py:639
  93.7 3.2 %finish.1 = (bf16[256,640]{1,0:T(8,128)(2,1)}, bf16[256,640]{1,0:T(8,128)(2,1)}, bf16[256,640]{1,0:T(8,128)(2,1)}, f32[3,640,128]{2,1,0:T(8,128)}, f32[3,128,640]{2,1,0:T(8,128)}) custom-call(bf16[256,640]{1,0:T(8,128)(2,1)} %get-tuple-element.9.q_in, bf16[256,640]{1,0:T(8,128)(2,1)} %get-tuple-element.10.k_in, bf16[256,640]{1,0:T(8,128)(2,1)} %get-tuple-element.11.v_in, ...), custom_call_target="tpu_custom_call" | custom-call | tf_op jit(solution)/shard_map/finish/pallas_call | solution.py:602
